TPU v7x, 32 devices: a whole 2x2x4 slice. The times are simulated.
32 devices in a mesh: pipe: 4 (over y, core), expert: 8 (over z, x).
Axes of the slice: x: 2, y: 2, z: 4, core: 2. Of those that a mesh axis runs over, the one named last changes fastest.
Arguments:
- forward_input: bfloat16 [4, 1024, 3584], P('pipe', 'expert'), may hold values from -6 to 6
- forward_route: int32 [4, 1024, 1], P('pipe', 'expert'), may hold values from 0 to 1; in each aligned block of 128 rows (0 to 127, 128 to 255, ..., all dimensions but the last counted through in order) at most 96 rows name the same one
- forward_weight: float32 [4, 1024, 1], P('pipe', 'expert'), may hold values from 0.3 to 3
- backward_input: bfloat16 [4, 1024, 3584], P('pipe', 'expert'), may hold values from -6 to 6
- backward_route: int32 [4, 1024, 1], P('pipe', 'expert'), may hold values from 0 to 1; in each aligned block of 128 rows (0 to 127, 128 to 255, ..., all dimensions but the last counted through in order) at most 96 rows name the same one
- backward_weight: float32 [4, 1024, 1], P('pipe', 'expert'), may hold values from 0.3 to 3
- output_grad: bfloat16 [4, 1024, 3584], P('pipe', 'expert'), may hold values from -6 to 6
- norm_gain: float32 [4, 3584], P('pipe'), may hold values from 0.1 to 1.9
- gate_weight: bfloat16 [4, 3584, 2048], P('pipe', None, 'expert'), may hold values from -0.09375 to 0.09375
- up_weight: bfloat16 [4, 3584, 2048], P('pipe', None, 'expert'), may hold values from -0.09375 to 0.09375
- down_weight: bfloat16 [4, 2048, 3584], P('pipe', 'expert'), may hold values from -0.1875 to 0.1875
Outputs:
- next_input: bfloat16 [4, 1024, 3584], P('pipe', 'expert')
- previous_grad: bfloat16 [4, 1024, 3584], P('pipe', 'expert')
Inputs may be any that keep to these rules, and one draw needn't show every extreme that they name: `forward_route`: each token is routed to exactly one expert. Among the 128 tokens of one device no expert is named more than 96 times, and in some device's tokens one expert is named exactly 96 times. `backward_route`: as forward_route.
All inputs are finite; a program needn't handle non-finite values.
Results may differ from a plain program's by a relative error of at most 0.0066.
Values may be sent and summed in bfloat16 or wider, within the bound.
A program may use at most 192 MiB of HBM per device.

v0:
```python
import jax
import jax.numpy as jnp
from jax import lax
from jax.sharding import PartitionSpec as P

HID = 1024


EPS = 1e-06


def passed_along(array, axis, by):
    devices = lax.axis_size(axis)
    return lax.ppermute(array, axis, [(i, (i + by) % devices) for i in range(devices)])


def normalize(values, gain):
    widened = values.astype(jnp.float32)
    scale = lax.rsqrt(jnp.mean(widened * widened, axis=-1, keepdims=True) + EPS)
    return (widened, scale, (widened * scale * gain).astype(jnp.bfloat16))


def slot_table(routes, experts, capacity):
    pairs = routes.shape[0] * routes.shape[1]
    flat = routes.reshape(-1)
    onehot = (flat[:, None] == jnp.arange(experts, dtype=jnp.int32)[None, :]).astype(jnp.int32)
    ranks = jnp.sum((jnp.cumsum(onehot, axis=0) - 1) * onehot, axis=1)
    target = flat * capacity + ranks
    owner = (
        jnp.full((experts * capacity,), pairs, jnp.int32)
        .at[target]
        .set(jnp.arange(pairs, dtype=jnp.int32))
    )
    return (target, owner)


def spread(table, owner, experts, group):
    picked = table[owner]
    width = picked.shape[-1]
    picked = picked.reshape(experts, 1, -1, width)
    picked = jnp.broadcast_to(picked, (experts, group, picked.shape[2], width))
    return picked.reshape(experts * group, -1, width)


def collect(returned, target, experts, group):
    width = returned.shape[-1]
    summed = jnp.sum(returned.reshape(experts, group, -1, width).astype(jnp.float32), axis=1)
    return summed.reshape(-1, width)[target]


def expert_forward(slots, gate_cols, up_cols, down_rows):
    leading = slots.shape[:2]
    flat = slots.reshape(-1, slots.shape[-1])
    gate_pre = jnp.dot(flat, gate_cols, preferred_element_type=jnp.float32)
    up_pre = jnp.dot(flat, up_cols, preferred_element_type=jnp.float32)
    hidden = (jax.nn.silu(gate_pre) * up_pre).astype(jnp.bfloat16)
    result = jnp.dot(hidden, down_rows, preferred_element_type=jnp.float32).astype(jnp.bfloat16)
    return result.reshape(leading + (result.shape[-1],))


def expert_backward(slots, grads, gate_cols, up_cols, down_rows):
    leading = slots.shape[:2]
    flat = slots.reshape(-1, slots.shape[-1])
    flat_grads = grads.reshape(-1, grads.shape[-1])
    gate_back = jnp.dot(flat, gate_cols, preferred_element_type=jnp.float32)
    up_back = jnp.dot(flat, up_cols, preferred_element_type=jnp.float32)
    contract = (((1,), (1,)), ((), ()))
    hidden_grad = lax.dot_general(
        flat_grads, down_rows, contract, preferred_element_type=jnp.float32
    )
    sigmoid_gate = jax.nn.sigmoid(gate_back)
    gate_grad = (
        hidden_grad * up_back * sigmoid_gate * (1.0 + gate_back * (1.0 - sigmoid_gate))
    ).astype(jnp.bfloat16)
    up_grad = (hidden_grad * gate_back * sigmoid_gate).astype(jnp.bfloat16)
    back = lax.dot_general(gate_grad, gate_cols, contract, preferred_element_type=jnp.float32)
    back = back + lax.dot_general(up_grad, up_cols, contract, preferred_element_type=jnp.float32)
    back = back.astype(jnp.bfloat16)
    return back.reshape(leading + (back.shape[-1],))


def per_device(
    forward_input,
    forward_route,
    forward_weight,
    backward_input,
    backward_route,
    backward_weight,
    output_grad,
    norm_gain,
    gate_weight,
    up_weight,
    down_weight,
):
    group = HID // gate_weight.shape[2]
    experts = lax.axis_size("expert") // group
    tokens = forward_input.shape[1]
    top = forward_route.shape[2]
    width = forward_input.shape[2]
    capacity = max(2, 3 * tokens * top // (2 * experts))
    gain = norm_gain[0]
    gate_cols, up_cols, down_rows = (gate_weight[0], up_weight[0], down_weight[0])
    ahead_wide, ahead_scale, ahead_normed = normalize(forward_input[0], gain)
    behind_wide, behind_scale, behind_normed = normalize(backward_input[0], gain)
    zero_row = jnp.zeros((1, width), jnp.bfloat16)
    cotangent = output_grad[0].astype(jnp.float32)
    routed_grad = (
        jnp.repeat(cotangent, top, axis=0) * backward_weight[0].reshape(-1)[:, None]
    ).astype(jnp.bfloat16)
    ahead_rows = jnp.concatenate([ahead_normed, zero_row], axis=0)
    behind_rows = jnp.concatenate([behind_normed, zero_row], axis=0)
    grad_rows = jnp.concatenate([routed_grad, zero_row], axis=0)
    ahead_target, ahead_owner = slot_table(forward_route[0], experts, capacity)
    behind_target, behind_owner = slot_table(backward_route[0], experts, capacity)
    ahead_send = spread(ahead_rows, ahead_owner // top, experts, group)
    behind_send = spread(behind_rows, behind_owner // top, experts, group)
    grad_send = spread(grad_rows, behind_owner, experts, group)
    ahead_part = expert_forward(
        lax.all_to_all(ahead_send, "expert", split_axis=0, concat_axis=0, tiled=True),
        gate_cols,
        up_cols,
        down_rows,
    )
    behind_part = expert_backward(
        lax.all_to_all(behind_send, "expert", split_axis=0, concat_axis=0, tiled=True),
        lax.all_to_all(grad_send, "expert", split_axis=0, concat_axis=0, tiled=True),
        gate_cols,
        up_cols,
        down_rows,
    )
    ahead_back, behind_back = (
        lax.all_to_all(ahead_part, "expert", split_axis=0, concat_axis=0, tiled=True),
        lax.all_to_all(behind_part, "expert", split_axis=0, concat_axis=0, tiled=True),
    )
    ahead_values = collect(ahead_back, ahead_target, experts, group)
    behind_values = collect(behind_back, behind_target, experts, group)
    mixed = jnp.sum(
        ahead_values.reshape(tokens, top, width) * forward_weight[0][:, :, None], axis=1
    )
    section_out = (ahead_wide + mixed).astype(jnp.bfloat16)
    normed_grad = jnp.sum(behind_values.reshape(tokens, top, width), axis=1)
    unit = behind_wide * behind_scale
    unit_grad = gain * normed_grad
    section_grad = cotangent + behind_scale * (
        unit_grad - unit * jnp.mean(unit_grad * unit, axis=-1, keepdims=True)
    )
    section_grad = section_grad.astype(jnp.bfloat16)
    next_input = passed_along(section_out, "pipe", 1)
    previous_grad = passed_along(section_grad, "pipe", -1)
    return (next_input[None], previous_grad[None])


def solution(mesh):
    return jax.shard_map(
        per_device,
        mesh=mesh,
        in_specs=(
            P("pipe", "expert", None),
            P("pipe", "expert", None),
            P("pipe", "expert", None),
            P("pipe", "expert", None),
            P("pipe", "expert", None),
            P("pipe", "expert", None),
            P("pipe", "expert", None),
            P("pipe", None),
            P("pipe", None, "expert"),
            P("pipe", None, "expert"),
            P("pipe", "expert", None),
        ),
        out_specs=(P("pipe", "expert", None), P("pipe", "expert", None)),
        check_vma=False,
    )
```

profile of v0, /device:TPU:1, one launch (start us, length us, event | category | flops | bytes accessed | tf_op | source)
XLA Modules:
  0.0 733.8 jit_solution(2661994019809450997)
XLA Ops:
  5.6 2.5 gather_fusion.3
  8.2 4.2 broadcast_in_dim.52
  12.4 6.5 all-to-all-start.3
  19.2 2.5 gather_fusion.2
  21.7 117.7 %all-to-all-done.3 = bf16[8,96,3584]{2,1,0:T(8,128)(2,1)} async-done(((bf16[8,96,3584]{2,1,0:T(8,128)(2,1)}), bf16[8,96,3584]{2,1,0:T(8,128)(2,1)}, u32[]{:S(2)}, u32[]{:S(2)}) %all-to-all-start.3) | async-done | bytes 5505056 | tf_op jit(solution)/shard_map/all_to_all | solution.py:125
  139.4 4.2 broadcast_in_dim.50
  143.6 4.9 all-to-all-start.2
  148.4 4.7 fusion.24
  153.2 114.8 %all-to-all-done.2 = bf16[8,96,3584]{2,1,0:T(8,128)(2,1)} async-done(((bf16[8,96,3584]{2,1,0:T(8,128)(2,1)}), bf16[8,96,3584]{2,1,0:T(8,128)(2,1)}, u32[]{:S(2)}, u32[]{:S(2)}) %all-to-all-start.2) | async-done | bytes 5505056 | tf_op jit(solution)/shard_map/all_to_all | solution.py:126
  268.0 4.7 fusion.14
  272.7 13.1 %fusion.22 = f32[768,3584]{1,0:T(8,128)} fusion(bf16[1,3584,256]{2,1,0:T(8,128)(2,1)} %param.19, f32[768,256]{1,0:T(8,128)S(1)} %fusion.14, bf16[768,3584]{1,0:T(8,128)(2,1)} %bitcast.31, bf16[1,3584,256]{2,1,0:T(8,128)(2,1)S(1)} %copy-done, f32[768,256]{1,0:T(8,128)S(1)} %fusion.24), kind=kOutput, calls=%fused_computation.40 | convolution fusion | flops 2820538368 | bytes 21757952 | tf_op jit(solution)/shard_map/dot_general | solution.py:76
  285.8 8.1 %add_convert_fusion = bf16[768,3584]{1,0:T(8,128)(2,1)} fusion(f32[768,3584]{1,0:T(8,128)} %fusion.22, bf16[1,3584,256]{2,1,0:T(8,128)(2,1)S(1)} %copy-done, f32[768,256]{1,0:T(8,128)S(1)} %fusion.14, f32[768,256]{1,0:T(8,128)S(1)} %fusion.24), kind=kOutput, calls=%fused_computation.9 | convolution fusion | flops 1415970816 | bytes 19922944 | tf_op jit(solution)/shard_map/dot_general | solution.py:77
  293.9 5.6 all-to-all-start.4
  301.3 118.0 %all-to-all-done.4 = bf16[8,96,3584]{2,1,0:T(8,128)(2,1)} async-done(((bf16[8,96,3584]{2,1,0:T(8,128)(2,1)}), bf16[8,96,3584]{2,1,0:T(8,128)(2,1)}, u32[]{:S(2)}, u32[]{:S(2)}) %all-to-all-start.4) | async-done | bytes 5505056 | tf_op jit(solution)/shard_map/all_to_all | solution.py:133
  419.3 5.2 convert_reduce_fusion
  424.5 5.1 gather_fusion.4
  429.6 2.1 fusion.6
  431.9 3.0 fusion.4
  435.0 2.5 gather_fusion
  437.5 1.8 broadcast_in_dim.22
  439.3 125.6 %all_to_all.25 = bf16[8,96,3584]{2,1,0:T(8,128)(2,1)S(1)} all-to-all(bf16[8,96,3584]{2,1,0:T(8,128)(2,1)S(1)} %bitcast.101), channel_id=1, replica_groups=mesh['pipe'=4,'expert'=8] {'expert'}, dimensions={0} | all-to-all | bytes 11010048 | tf_op jit(solution)/shard_map/all_to_all | solution.py:119
  564.9 2.4 copy-done.6
  568.9 11.4 %convolution_convert_fusion = bf16[768,3584]{1,0:T(8,128)(2,1)} fusion(bf16[1,256,3584]{2,1,0:T(8,128)(2,1)} %param.21, bf16[768,3584]{1,0:T(8,128)(2,1)} %bitcast.107, bf16[1,3584,256]{2,1,0:T(8,128)(2,1)S(1)} %copy-done, f32[768,256]{1,0:T(8,128)S(1)} %fusion.26), kind=kOutput, calls=%fused_computation.10 | convolution fusion | flops 2822504448 | bytes 15466496 | tf_op jit(solution)/shard_map/dot_general | solution.py:57
  580.2 4.7 all-to-all-start.1
  584.9 2.3 collective-permute-start.1
  587.2 117.1 %all-to-all-done.1 = bf16[8,96,3584]{2,1,0:T(8,128)(2,1)} async-done(((bf16[8,96,3584]{2,1,0:T(8,128)(2,1)}), bf16[8,96,3584]{2,1,0:T(8,128)(2,1)}, u32[]{:S(2)}, u32[]{:S(2)}) %all-to-all-start.1) | async-done | bytes 5505056 | tf_op jit(solution)/shard_map/all_to_all | solution.py:132
  704.3 5.2 convert_reduce_fusion.1
  709.5 5.1 gather_fusion.1
  714.6 1.8 fusion.13
  716.4 4.0 collective-permute-start
  720.4 10.3 %collective-permute-done = bf16[128,3584]{1,0:T(8,128)(2,1)S(1)} collective-permute-done((bf16[128,3584]{1,0:T(8,128)(2,1)S(1)}, bf16[128,3584]{1,0:T(8,128)(2,1)S(1)}, u32[]{:S(2)}, u32[]{:S(2)}) %collective-permute-start) | collective-permute-done | bytes 917536 | tf_op jit(solution)/shard_map/ppermute | solution.py:14
  731.7 2.2 copy.16
  (58 shorter events, 9.6 us)
Async XLA Ops:
  0.6 272.1 %copy-start = (bf16[1,3584,256]{2,1,0:T(8,128)(2,1)S(1)}, bf16[1,3584,256]{2,1,0:T(8,128)(2,1)}, u32[]{:S(2)}) copy-start(bf16[1,3584,256]{2,1,0:T(8,128)(2,1)} %param.20) | copy-start | bytes 5505028
  0.6 4.6 copy-start.2
  0.7 3.1 copy-start.10
  0.7 4.5 copy-start.9
  12.4 6.5 copy-start.7
  12.4 6.5 copy-start.12
  12.4 127.0 %all-to-all-start.3 = ((bf16[8,96,3584]{2,1,0:T(8,128)(2,1)}), bf16[8,96,3584]{2,1,0:T(8,128)(2,1)}, u32[]{:S(2)}, u32[]{:S(2)}) async-start(bf16[8,96,3584]{2,1,0:T(8,128)(2,1)} %bitcast.99), calls=%async_computation.3 | async-start | bytes 11010048 | tf_op jit(solution)/shard_map/all_to_all | solution.py:125
  143.6 124.4 %all-to-all-start.2 = ((bf16[8,96,3584]{2,1,0:T(8,128)(2,1)}), bf16[8,96,3584]{2,1,0:T(8,128)(2,1)}, u32[]{:S(2)}, u32[]{:S(2)}) async-start(bf16[8,96,3584]{2,1,0:T(8,128)(2,1)} %bitcast.100), calls=%async_computation.2 | async-start | bytes 11010048 | tf_op jit(solution)/shard_map/all_to_all | solution.py:126
  293.9 5.6 copy-start.11
  293.9 125.4 %all-to-all-start.4 = ((bf16[8,96,3584]{2,1,0:T(8,128)(2,1)}), bf16[8,96,3584]{2,1,0:T(8,128)(2,1)}, u32[]{:S(2)}, u32[]{:S(2)}) async-start(bf16[8,96,3584]{2,1,0:T(8,128)(2,1)} %bitcast.98), calls=%async_computation.4 | async-start | bytes 11010048 | tf_op jit(solution)/shard_map/all_to_all | solution.py:133
  424.5 5.1 copy-start.3
  429.6 2.1 copy-start.1
  429.6 2.3 copy-start.4
  439.3 128.0 %copy-start.8 = (bf16[1,3584,256]{2,1,0:T(8,128)(2,1)S(1)}, bf16[1,3584,256]{2,1,0:T(8,128)(2,1)}, u32[]{:S(2)}) copy-start(bf16[1,3584,256]{2,1,0:T(8,128)(2,1)} %param.19) | copy-start | bytes 5505028
  564.9 2.4 copy-start.6
  580.2 124.1 %all-to-all-start.1 = ((bf16[8,96,3584]{2,1,0:T(8,128)(2,1)}), bf16[8,96,3584]{2,1,0:T(8,128)(2,1)}, u32[]{:S(2)}, u32[]{:S(2)}) async-start(bf16[8,96,3584]{2,1,0:T(8,128)(2,1)} %bitcast.105), calls=%async_computation.1 | async-start | bytes 11010048 | tf_op jit(solution)/shard_map/all_to_all | solution.py:132
  584.9 135.5 %collective-permute-start.1 = (bf16[128,3584]{1,0:T(8,128)(2,1)}, bf16[128,3584]{1,0:T(8,128)(2,1)}, u32[]{:S(2)}, u32[]{:S(2)}) collective-permute-start(bf16[128,3584]{1,0:T(8,128)(2,1)} %get-tuple-element.2), channel_id=1, source_target_pairs={{0,24},{8,0},{16,8},{24,16},{1,25},{9,1},{17,9},{25,17},{2,26},{10... | collective-permute-start | bytes 2752520 | tf_op jit(solution)/shard_map/ppermute | solution.py:14
  709.5 5.1 copy-start.5
  709.5 5.1 copy-start.13
  716.4 14.3 %collective-permute-start = (bf16[128,3584]{1,0:T(8,128)(2,1)S(1)}, bf16[128,3584]{1,0:T(8,128)(2,1)S(1)}, u32[]{:S(2)}, u32[]{:S(2)}) collective-permute-start(bf16[128,3584]{1,0:T(8,128)(2,1)S(1)} %fusion.13), channel_id=1, source_target_pairs={{0,8},{8,16},{16,24},{24,0},{1,9},{9,17},{17,25},{25,1},{2,10},{10... | collective-permute-start | bytes 2752520 | tf_op jit(solution)/shard_map/ppermute | solution.py:14
where the time goes:
time: 736 us; the launch traced here: 734 us
  waiting for transfers between devices  478 us (65%)
  blocking collectives  126 us (17%)
  matrix products  43.6 us (6%)
  local copies, waits for them, and re-layouts  36 us (5%)
  starting transfers between devices  27.9 us (4%)
  other arithmetic  21.8 us (3%)
    all_to_all x1, blocking collectives, per_device(): lax.all_to_all(ahead_send, 'expert', split_axis=0, concat_axis=0, tiled=T...  126 us
    all_to_all x1, waiting for transfers between devices, per_device(): lax.all_to_all(behind_part, 'expert', split_axis=0, concat_axis=0, tiled=...  118 us
    all_to_all x1, waiting for transfers between devices, per_device(): lax.all_to_all(behind_send, 'expert', split_axis=0, concat_axis=0, tiled=...  118 us
    all_to_all x1, waiting for transfers between devices, per_device(): lax.all_to_all(ahead_part, 'expert', split_axis=0, concat_axis=0, tiled=T...  117 us
    all_to_all x1, waiting for transfers between devices, per_device(): lax.all_to_all(grad_send, 'expert', split_axis=0, concat_axis=0, tiled=True)  115 us
  transfers between devices with their start and end apart: 6, of which 5 were waited for; matrix products, arithmetic and copies ran while one was open for 3% of the time, Pallas kernels for 0%

commit v1 on v0

v1 whole, which is shorter than its diff:
```python
import jax
import jax.numpy as jnp
from jax import lax
from jax.sharding import PartitionSpec as P

HID = 1024


EPS = 1e-06


def passed_along(array, axis, by):
    devices = lax.axis_size(axis)
    return lax.ppermute(array, axis, [(i, (i + by) % devices) for i in range(devices)])


def swapped(array, bit):
    devices = lax.axis_size("expert")
    return lax.ppermute(array, "expert", [(i, i ^ bit) for i in range(devices)])


def normalize(values, gain):
    widened = values.astype(jnp.float32)
    scale = lax.rsqrt(jnp.mean(widened * widened, axis=-1, keepdims=True) + EPS)
    return (widened, scale, (widened * scale * gain).astype(jnp.bfloat16))


def slot_matrix(routes, experts, capacity, mine):
    flat = lax.rem(routes.reshape(-1) + (experts - mine), experts)
    pairs = flat.shape[0]
    onehot = flat[:, None] == jnp.arange(experts, dtype=jnp.int32)[None, :]
    before = jnp.arange(pairs)[:, None] > jnp.arange(pairs)[None, :]
    counts = jnp.dot(
        before.astype(jnp.bfloat16), onehot.astype(jnp.bfloat16), preferred_element_type=jnp.float32
    )
    ranks = jnp.sum(jnp.where(onehot, counts, 0.0), axis=1).astype(jnp.int32)
    target = flat * capacity + ranks
    slots = jnp.arange(experts * capacity, dtype=jnp.int32)
    return (slots[:, None] == target[None, :]).astype(jnp.bfloat16)


def to_slots(matrix, rows):
    return jnp.dot(matrix, rows, preferred_element_type=jnp.float32).astype(jnp.bfloat16)


def from_slots(matrix, rows):
    return lax.dot_general(
        matrix, rows, (((0,), (0,)), ((), ())), preferred_element_type=jnp.float32
    )


def across(slots, experts, group, sign):
    blocks = jnp.split(slots, experts, axis=0)
    return blocks[:1] + [
        passed_along(blocks[k], "expert", sign * group * k) for k in range(1, experts)
    ]


def dot(a, b):
    return jnp.dot(a, b, preferred_element_type=jnp.float32)


def dot_t(a, b):
    return lax.dot_general(a, b, (((1,), (1,)), ((), ())), preferred_element_type=jnp.float32)


def forward_sum(rows, weights):
    total = None
    for gate, up, down in weights:
        hidden = (jax.nn.silu(dot(rows, gate)) * dot(rows, up)).astype(jnp.bfloat16)
        part = dot(hidden, down)
        total = part if total is None else total + part
    return total


def backward_sum(rows, grads, weights):
    total = None
    for gate, up, down in weights:
        gate_back = dot(rows, gate)
        up_back = dot(rows, up)
        hidden_grad = dot_t(grads, down)
        sig = jax.nn.sigmoid(gate_back)
        gate_grad = (hidden_grad * up_back * sig * (1.0 + gate_back * (1.0 - sig))).astype(
            jnp.bfloat16
        )
        up_grad = (hidden_grad * gate_back * sig).astype(jnp.bfloat16)
        part = dot_t(gate_grad, gate) + dot_t(up_grad, up)
        total = part if total is None else total + part
    return total


def per_device(
    forward_input,
    forward_route,
    forward_weight,
    backward_input,
    backward_route,
    backward_weight,
    output_grad,
    norm_gain,
    gate_weight,
    up_weight,
    down_weight,
):
    group = HID // gate_weight.shape[2]
    assert group == 4
    experts = lax.axis_size("expert") // group
    tokens = forward_input.shape[1]
    top = forward_route.shape[2]
    width = forward_input.shape[2]
    capacity = max(2, 3 * tokens * top // (2 * experts))
    mine = lax.axis_index("expert") // group
    gain = norm_gain[0]
    own = (gate_weight[0], up_weight[0], down_weight[0])
    other = tuple(swapped(w, 2) for w in own)
    weights = (own, other)

    ahead_wide, ahead_scale, ahead_normed = normalize(forward_input[0], gain)
    behind_wide, behind_scale, behind_normed = normalize(backward_input[0], gain)
    cotangent = output_grad[0].astype(jnp.float32)
    routed_grad = (
        jnp.repeat(cotangent, top, axis=0) * backward_weight[0].reshape(-1)[:, None]
    ).astype(jnp.bfloat16)
    ahead_slots = slot_matrix(forward_route[0], experts, capacity, mine)
    behind_slots = slot_matrix(backward_route[0], experts, capacity, mine)

    def gathered(matrix, rows):
        pieces = across(to_slots(matrix, rows), experts, group, 1)
        near = jnp.concatenate(pieces, axis=0)
        far = jnp.concatenate(
            [swapped(pieces[0], 1), swapped(jnp.concatenate(pieces[1:], axis=0), 1)], axis=0
        )
        return near, far

    def returned(near_sum, far_sum):
        total = (near_sum + swapped(far_sum.astype(jnp.bfloat16), 1)).astype(jnp.bfloat16)
        return jnp.concatenate(across(total, experts, group, -1), axis=0)

    ahead_near, ahead_far = gathered(ahead_slots, jnp.repeat(ahead_normed, top, axis=0))
    behind_near, behind_far = gathered(behind_slots, jnp.repeat(behind_normed, top, axis=0))
    grad_near, grad_far = gathered(behind_slots, routed_grad)

    ahead_back = returned(forward_sum(ahead_near, weights), forward_sum(ahead_far, weights))
    ahead_values = from_slots(ahead_slots, ahead_back)
    mixed = jnp.sum(
        ahead_values.reshape(tokens, top, width) * forward_weight[0][:, :, None], axis=1
    )
    section_out = (ahead_wide + mixed).astype(jnp.bfloat16)
    next_input = passed_along(section_out, "pipe", 1)

    behind_back = returned(
        backward_sum(behind_near, grad_near, weights), backward_sum(behind_far, grad_far, weights)
    )
    behind_values = from_slots(behind_slots, behind_back)
    normed_grad = jnp.sum(behind_values.reshape(tokens, top, width), axis=1)
    unit = behind_wide * behind_scale
    unit_grad = gain * normed_grad
    section_grad = cotangent + behind_scale * (
        unit_grad - unit * jnp.mean(unit_grad * unit, axis=-1, keepdims=True)
    )
    section_grad = section_grad.astype(jnp.bfloat16)
    previous_grad = passed_along(section_grad, "pipe", -1)
    return (next_input[None], previous_grad[None])


def solution(mesh):
    return jax.shard_map(
        per_device,
        mesh=mesh,
        in_specs=(
            P("pipe", "expert", None),
            P("pipe", "expert", None),
            P("pipe", "expert", None),
            P("pipe", "expert", None),
            P("pipe", "expert", None),
            P("pipe", "expert", None),
            P("pipe", "expert", None),
            P("pipe", None),
            P("pipe", None, "expert"),
            P("pipe", None, "expert"),
            P("pipe", "expert", None),
        ),
        out_specs=(P("pipe", "expert", None), P("pipe", "expert", None)),
        check_vma=False,
    )
```

time: 736 us -> 370 us (0.50)
  waiting for transfers between devices: 478 us -> 214 us
  blocking collectives: 126 us -> 0 us
  matrix products: 43.6 us -> 94.8 us
  local copies, waits for them, and re-layouts: 36 us -> 13.7 us
  other arithmetic: 21.8 us -> 4.45 us
  starting transfers between devices: 27.9 us -> 40.1 us
    all_to_all x4 -> x0, waiting for transfers between devices: 468 us -> none  [the longest x1 118 us: per_device(): lax.all_to_all(behind_part, 'expert', split_axis=0, concat_axis=0, tiled=...]
    ppermute x2 -> x7, waiting for transfers between devices: 10.3 us -> 150 us  [passed_along(): lax.ppermute(array, axis, [(i, (i + by) % devices) for i in range(devices)])]
    all_to_all x1 -> x0, blocking collectives: 126 us -> none  [per_device(): lax.all_to_all(ahead_send, 'expert', split_axis=0, concat_axis=0, tiled=T...]
    ppermute x0 -> x11, waiting for transfers between devices: none -> 64.1 us  [swapped(): return lax.ppermute(array, 'expert', [(i, i ^ bit) for i in range(devices)])]
    dot_general x6 -> x31, matrix products: 43.6 us -> 94.8 us  [the longest x12 46.7 us: dot_t(): lax.dot_general(a, b, (((1,), (1,)), ((), ())), preferred_element_type=jn...]
    ppermute x2 -> x7, starting transfers between devices: 6.26 us -> 30.4 us  [passed_along(): lax.ppermute(array, axis, [(i, (i + by) % devices) for i in range(devices)])]
    all_to_all x4 -> x0, starting transfers between devices: 21.7 us -> none  [the longest x1 6.49 us: per_device(): lax.all_to_all(behind_send, 'expert', split_axis=0, concat_axis=0, tiled=...]
    gather x5 -> x0, local copies, waits for them, and re-layouts: 17.7 us -> none  [the longest x2 10.1 us: collect(): return summed.reshape(-1, width)[target]]
  transfers between devices with their start and end apart: 6 -> 18, of which waited for: 5 -> 12; matrix products, arithmetic and copies ran while one was open for 3% -> 25% of each run, Pallas kernels for 0% -> 0%
where the time goes in v1:
time: 370 us; the launch traced here: 368 us
  waiting for transfers between devices  214 us (58%)
  matrix products  94.8 us (26%)
  starting transfers between devices  40.1 us (11%)
  local copies, waits for them, and re-layouts  13.7 us (4%)
  other arithmetic  4.45 us (1%)
    ppermute x7, waiting for transfers between devices, passed_along(): lax.ppermute(array, axis, [(i, (i + by) % devices) for i in range(devices)])  150 us
    ppermute x11, waiting for transfers between devices, swapped(): return lax.ppermute(array, 'expert', [(i, i ^ bit) for i in range(devices)])  64.1 us
    dot_general x12, matrix products, dot_t(): lax.dot_general(a, b, (((1,), (1,)), ((), ())), preferred_element_type=jn...  46.7 us
    dot_general x12, matrix products, dot(): return jnp.dot(a, b, preferred_element_type=jnp.float32)  42.5 us
    ppermute x7, starting transfers between devices, passed_along(): lax.ppermute(array, axis, [(i, (i + by) % devices) for i in range(devices)])  30.4 us
    ppermute x11, starting transfers between devices, swapped(): return lax.ppermute(array, 'expert', [(i, i ^ bit) for i in range(devices)])  9.67 us
  transfers between devices with their start and end apart: 18, of which 12 were waited for; matrix products, arithmetic and copies ran while one was open for 25% of the time, Pallas kernels for 0%

profile of v1, /device:TPU:1, one launch (start us, length us, event | category | flops | bytes accessed | tf_op | source)
XLA Modules:
  0.0 368.3 jit_solution(2774948349130600370)
XLA Ops:
  16.3 7.3 %collective-permute-done.13 = bf16[96,3584]{1,0:T(8,128)(2,1)S(1)} collective-permute-done((bf16[96,3584]{1,0:T(8,128)(2,1)S(1)}, bf16[96,3584]{1,0:T(8,128)(2,1)S(1)}, u32[]{:S(2)}, u32[]{:S(2)}) %collective-permute-start.13) | collective-permute-done | bytes 688160 | tf_op jit(solution)/shard_map/ppermute | solution.py:19
  24.9 30.3 %collective-permute-done.10 = bf16[96,3584]{1,0:T(8,128)(2,1)} collective-permute-done((bf16[96,3584]{1,0:T(8,128)(2,1)S(1)}, bf16[96,3584]{1,0:T(8,128)(2,1)}, u32[]{:S(2)}, u32[]{:S(2)}) %collective-permute-start.10) | collective-permute-done | bytes 688160 | tf_op jit(solution)/shard_map/ppermute | solution.py:14
  60.0 9.8 %collective-permute-done.9 = bf16[96,3584]{1,0:T(8,128)(2,1)S(1)} collective-permute-done((bf16[96,3584]{1,0:T(8,128)(2,1)S(1)}, bf16[96,3584]{1,0:T(8,128)(2,1)S(1)}, u32[]{:S(2)}, u32[]{:S(2)}) %collective-permute-start.9) | collective-permute-done | bytes 688160 | tf_op jit(solution)/shard_map/ppermute | solution.py:14
  70.7 2.9 fusion.57
  73.7 5.4 %fusion.42 = f32[192,3584]{1,0:T(8,128)} fusion(f32[192,256]{1,0:T(8,128)} %fusion.57, f32[192,256]{1,0:T(8,128)S(1)} %fusion.130, bf16[1,3584,256]{2,1,0:T(8,128)(2,1)S(1)} %copy-done, bf16[1,3584,256]{2,1,0:T(8,128)(2,1)} %param.19, bf16[96,3584]{1,0:T(8,128)(2,1)} %collective-permute-done.10, bf16[96,3584]{1,0:T(8,128)(2,1)} %copy-done.8), kind=kOutput, calls=%fused_computation.66 | convolution fusion | flops 707887104 | bytes 8192000 | tf_op jit(solution)/shard_map/dot_general | solution.py:64
  79.1 4.3 %convolution_add_fusion.3 = f32[192,3584]{1,0:T(8,128)} fusion(f32[192,3584]{1,0:T(8,128)} %fusion.42, f32[192,256]{1,0:T(8,128)} %fusion.57, f32[192,256]{1,0:T(8,128)S(1)} %fusion.130, bf16[1,3584,256]{2,1,0:T(8,128)(2,1)S(1)} %copy-done), kind=kOutput, calls=%fused_computation.6 | convolution fusion | flops 353304576 | bytes 7733248 | tf_op jit(solution)/shard_map/dot_general | solution.py:64
  83.3 88.7 %collective-permute-done = bf16[96,3584]{1,0:T(8,128)(2,1)} collective-permute-done((bf16[96,3584]{1,0:T(8,128)(2,1)}, bf16[96,3584]{1,0:T(8,128)(2,1)}, u32[]{:S(2)}, u32[]{:S(2)}) %collective-permute-start) | collective-permute-done | bytes 688160 | tf_op jit(solution)/shard_map/ppermute | solution.py:14
  172.3 2.5 fusion.134
  174.8 5.1 %fusion.70 = f32[192,3584]{1,0:T(8,128)} fusion(f32[192,256]{1,0:T(8,128)S(1)} %fusion.134, bf16[1,256,3584]{2,1,0:T(8,128)(2,1)} %param.21, bf16[1,3584,256]{2,1,0:T(8,128)(2,1)S(1)} %copy-done, bf16[96,3584]{1,0:T(8,128)(2,1)} %collective-permute-done, bf16[96,3584]{1,0:T(8,128)(2,1)} %get-tuple-element.10), kind=kOutput, calls=%fused_computation.105 | convolution fusion | flops 707690496 | bytes 7995392 | tf_op jit(solution)/shard_map/dot_general | solution.py:60
  183.1 4.3 %collective-permute-done.14 = bf16[96,3584]{1,0:T(8,128)(2,1)} collective-permute-done((bf16[96,3584]{1,0:T(8,128)(2,1)}, bf16[96,3584]{1,0:T(8,128)(2,1)}, u32[]{:S(2)}, u32[]{:S(2)}) %collective-permute-start.14) | collective-permute-done | bytes 688160 | tf_op jit(solution)/shard_map/ppermute | solution.py:19
  191.0 11.1 %collective-permute-done.12 = bf16[96,3584]{1,0:T(8,128)(2,1)S(1)} collective-permute-done((bf16[96,3584]{1,0:T(8,128)(2,1)}, bf16[96,3584]{1,0:T(8,128)(2,1)S(1)}, u32[]{:S(2)}, u32[]{:S(2)}) %collective-permute-start.12) | collective-permute-done | bytes 688160 | tf_op jit(solution)/shard_map/ppermute | solution.py:19
  202.2 14.7 %collective-permute-done.5 = bf16[96,3584]{1,0:T(8,128)(2,1)S(1)} collective-permute-done((bf16[96,3584]{1,0:T(8,128)(2,1)}, bf16[96,3584]{1,0:T(8,128)(2,1)S(1)}, u32[]{:S(2)}, u32[]{:S(2)}) %collective-permute-start.5) | collective-permute-done | bytes 688160 | tf_op jit(solution)/shard_map/ppermute | solution.py:19
  217.8 2.9 fusion.103
  220.7 5.0 %fusion.41 = f32[192,3584]{1,0:T(8,128)} fusion(f32[192,256]{1,0:T(8,128)} %fusion.103, bf16[192,3584]{1,0:T(8,128)(2,1)S(1)} %constant_dynamic-update-slice_fusion.4, f32[192,256]{1,0:T(8,128)S(1)} %fusion.127, bf16[1,3584,256]{2,1,0:T(8,128)(2,1)S(1)} %copy-done, bf16[1,3584,256]{2,1,0:T(8,128)(2,1)} %param.19), kind=kOutput, calls=%fused_computation.65 | convolution fusion | flops 705134592 | bytes 8192000 | tf_op jit(solution)/shard_map/dot_general | solution.py:64
  225.6 3.3 fusion.132
  231.3 5.2 %fusion.71 = f32[192,3584]{1,0:T(8,128)} fusion(f32[192,256]{1,0:T(8,128)} %fusion.132, bf16[1,256,3584]{2,1,0:T(8,128)(2,1)} %param.21, bf16[192,3584]{1,0:T(8,128)(2,1)} %constant_dynamic-update-slice_fusion, bf16[1,3584,256]{2,1,0:T(8,128)(2,1)S(1)} %copy-done), kind=kOutput, calls=%fused_computation.106 | convolution fusion | flops 704937984 | bytes 7995392 | tf_op jit(solution)/shard_map/dot_general | solution.py:60
  241.8 3.9 %fusion.73 = f32[192,3584]{1,0:T(8,128)} fusion(bf16[3584,256]{1,0:T(8,128)(2,1)} %collective-permute-done.2, f32[192,256]{1,0:T(8,128)S(1)} %fusion.159, f32[192,256]{1,0:T(8,128)S(1)} %fusion.160), kind=kOutput, calls=%fused_computation.108 | convolution fusion | flops 352616448 | bytes 4980736 | tf_op jit(solution)/shard_map/dot_general | solution.py:64
  245.7 6.7 %fusion.7 = bf16[192,3584]{1,0:T(8,128)(2,1)} fusion(f32[192,3584]{1,0:T(8,128)} %convolution_add_fusion.1, f32[192,3584]{1,0:T(8,128)} %fusion.73, bf16[3584,256]{1,0:T(8,128)(2,1)} %collective-permute-done.1, f32[192,256]{1,0:T(8,128)} %copy-done.14, bf16[192,3584]{1,0:T(8,128)(2,1)S(1)} %constant_dynamic-update-slice_fusion.4, ...), kind=kOutput, calls=%fused_computation.13 | convolution fusion | flops 707198976 | bytes 12320768 | tf_op jit(solution)/shard_map/dot_general | solution.py:64
  252.6 3.3 fusion.158
  255.9 5.4 %fusion.5 = bf16[192,3584]{1,0:T(8,128)(2,1)} fusion(f32[192,3584]{1,0:T(8,128)S(1)} %copy-done.2, bf16[256,3584]{1,0:T(8,128)(2,1)} %collective-permute-done.3, f32[192,256]{1,0:T(8,128)} %fusion.158, bf16[192,3584]{1,0:T(8,128)(2,1)} %constant_dynamic-update-slice_fusion, bf16[3584,256]{1,0:T(8,128)(2,1)} %collective-permute-done.2), kind=kOutput, calls=%fused_computation.11 | convolution fusion | flops 706314240 | bytes 9371648 | tf_op jit(solution)/shard_map/dot_general | solution.py:60
  267.0 3.2 fusion.149
  272.4 9.2 %collective-permute-done.15 = bf16[192,3584]{1,0:T(8,128)(2,1)} collective-permute-done((bf16[192,3584]{1,0:T(8,128)(2,1)}, bf16[192,3584]{1,0:T(8,128)(2,1)}, u32[]{:S(2)}, u32[]{:S(2)}) %collective-permute-start.15) | collective-permute-done | bytes 1376288 | tf_op jit(solution)/shard_map/ppermute | solution.py:19
  281.6 6.5 %fusion.6 = bf16[192,3584]{1,0:T(8,128)(2,1)} fusion(f32[192,3584]{1,0:T(8,128)} %convolution_add_fusion.3, f32[192,3584]{1,0:T(8,128)S(1)} %fusion.72, bf16[3584,256]{1,0:T(8,128)(2,1)} %collective-permute-done.1, bf16[192,3584]{1,0:T(8,128)(2,1)} %collective-permute-done.15, f32[192,256]{1,0:T(8,128)} %copy-done.17, ...), kind=kOutput, calls=%fused_computation.12 | convolution fusion | flops 711327744 | bytes 13697024 | tf_op jit(solution)/shard_map/dot_general | solution.py:64
  288.1 2.4 fusion.151
  290.5 3.1 collective-permute-start.16
  293.6 17.5 %collective-permute-done.6 = bf16[192,3584]{1,0:T(8,128)(2,1)} collective-permute-done((bf16[192,3584]{1,0:T(8,128)(2,1)}, bf16[192,3584]{1,0:T(8,128)(2,1)}, u32[]{:S(2)}, u32[]{:S(2)}) %collective-permute-start.6) | collective-permute-done | bytes 1376288 | tf_op jit(solution)/shard_map/ppermute | solution.py:19
  311.1 5.7 %fusion.4 = bf16[192,3584]{1,0:T(8,128)(2,1)} fusion(f32[192,3584]{1,0:T(8,128)S(1)} %copy-done.1, bf16[256,3584]{1,0:T(8,128)(2,1)} %collective-permute-done.3, bf16[192,3584]{1,0:T(8,128)(2,1)} %collective-permute-done.6, f32[192,256]{1,0:T(8,128)} %fusion.149, bf16[3584,256]{1,0:T(8,128)(2,1)} %collective-permute-done.1, ...), kind=kOutput, calls=%fused_computation.10 | convolution fusion | flops 710443008 | bytes 10747904 | tf_op jit(solution)/shard_map/dot_general | solution.py:60
  318.2 3.2 collective-permute-start.7
  325.7 17.9 %collective-permute-start.17 = (bf16[128,3584]{1,0:T(8,128)(2,1)S(1)}, bf16[128,3584]{1,0:T(8,128)(2,1)S(1)}, u32[]{:S(2)}, u32[]{:S(2)}) collective-permute-start(bf16[128,3584]{1,0:T(8,128)(2,1)S(1)} %fusion.14), channel_id=1, source_target_pairs={{0,24},{8,0},{16,8},{24,16},{1,25},{9,1},{17,9},{25,17},{2,26},{10... | collective-permute-start | bytes 2752520 | tf_op jit(solution)/shard_map/ppermute | solution.py:14
  343.6 9.0 %collective-permute-done.7 = bf16[96,3584]{1,0:T(8,128)(2,1)S(1)} collective-permute-done((bf16[96,3584]{1,0:T(8,128)(2,1)S(1)}, bf16[96,3584]{1,0:T(8,128)(2,1)S(1)}, u32[]{:S(2)}, u32[]{:S(2)}) %collective-permute-start.7) | collective-permute-done | bytes 688160 | tf_op jit(solution)/shard_map/ppermute | solution.py:14
  353.1 2.9 collective-permute-start.8
  356.1 10.3 %collective-permute-done.8 = bf16[128,3584]{1,0:T(8,128)(2,1)S(1)} collective-permute-done((bf16[128,3584]{1,0:T(8,128)(2,1)S(1)}, bf16[128,3584]{1,0:T(8,128)(2,1)S(1)}, u32[]{:S(2)}, u32[]{:S(2)}) %collective-permute-start.8) | collective-permute-done | bytes 917536 | tf_op jit(solution)/shard_map/ppermute | solution.py:14
  (109 shorter events, 54.3 us)
Async XLA Ops:
  6.1 4.6 %copy-start.10 = (bf16[1,128,3584]{2,1,0:T(8,128)(2,1)S(1)}, bf16[1,128,3584]{2,1,0:T(8,128)(2,1)}, u32[]{:S(2)}) copy-start(bf16[1,128,3584]{2,1,0:T(8,128)(2,1)} %param.17) | copy-start | bytes 2752516
  6.2 4.5 %copy-start.21 = (f32[1,128,1]{1,2,0:T(1,128)S(1)}, f32[1,128,1]{1,2,0:T(1,128)}, u32[]{:S(2)}) copy-start(f32[1,128,1]{1,2,0:T(1,128)} %param.16) | copy-start | bytes 1540
  6.3 50.3 %copy-start.8 = (bf16[96,3584]{1,0:T(8,128)(2,1)}, bf16[96,3584]{1,0:T(8,128)(2,1)S(1)}, u32[]{:S(2)}) copy-start(bf16[96,3584]{1,0:T(8,128)(2,1)S(1)} %get-tuple-element.4) | copy-start | bytes 2064388
  6.3 17.4 %collective-permute-start.13 = (bf16[96,3584]{1,0:T(8,128)(2,1)S(1)}, bf16[96,3584]{1,0:T(8,128)(2,1)S(1)}, u32[]{:S(2)}, u32[]{:S(2)}) collective-permute-start(bf16[96,3584]{1,0:T(8,128)(2,1)S(1)} %get-tuple-element.4), channel_id=1, source_target_pairs={{0,1},{1,0},{2,3},{3,2},{4,5},{5,4},{6,7},{7,6},{8,9},{9,8},{10,11... | collective-permute-start | bytes 2064392 | tf_op jit(solution)/shard_map/ppermute | solution.py:19
  8.4 46.8 %collective-permute-start.10 = (bf16[96,3584]{1,0:T(8,128)(2,1)S(1)}, bf16[96,3584]{1,0:T(8,128)(2,1)}, u32[]{:S(2)}, u32[]{:S(2)}) collective-permute-start(bf16[96,3584]{1,0:T(8,128)(2,1)S(1)} %get-tuple-element.5), channel_id=1, source_target_pairs={{0,4},{1,5},{2,6},{3,7},{4,0},{5,1},{6,2},{7,3},{8,12},{9,13},{10,... | collective-permute-start | bytes 2064392 | tf_op jit(solution)/shard_map/ppermute | solution.py:14
  11.4 58.4 %copy-start.18 = (bf16[96,3584]{1,0:T(8,128)(2,1)}, bf16[96,3584]{1,0:T(8,128)(2,1)S(1)}, u32[]{:S(2)}) copy-start(bf16[96,3584]{1,0:T(8,128)(2,1)S(1)} %get-tuple-element.6) | copy-start | bytes 2064388
  11.4 47.4 %collective-permute-start.11 = (bf16[96,3584]{1,0:T(8,128)(2,1)S(1)}, bf16[96,3584]{1,0:T(8,128)(2,1)S(1)}, u32[]{:S(2)}, u32[]{:S(2)}) collective-permute-start(bf16[96,3584]{1,0:T(8,128)(2,1)S(1)} %get-tuple-element.6), channel_id=1, source_target_pairs={{0,1},{1,0},{2,3},{3,2},{4,5},{5,4},{6,7},{7,6},{8,9},{9,8},{10,11... | collective-permute-start | bytes 2064392 | tf_op jit(solution)/shard_map/ppermute | solution.py:19
  11.8 58.1 %collective-permute-start.9 = (bf16[96,3584]{1,0:T(8,128)(2,1)S(1)}, bf16[96,3584]{1,0:T(8,128)(2,1)S(1)}, u32[]{:S(2)}, u32[]{:S(2)}) collective-permute-start(bf16[96,3584]{1,0:T(8,128)(2,1)S(1)} %get-tuple-element.7), channel_id=1, source_target_pairs={{0,4},{1,5},{2,6},{3,7},{4,0},{5,1},{6,2},{7,3},{8,12},{9,13},{10,... | collective-permute-start | bytes 2064392 | tf_op jit(solution)/shard_map/ppermute | solution.py:14
  12.7 223.8 %collective-permute-start.1 = (bf16[3584,256]{1,0:T(8,128)(2,1)}, bf16[3584,256]{1,0:T(8,128)(2,1)}, u32[]{:S(2)}, u32[]{:S(2)}) collective-permute-start(bf16[3584,256]{1,0:T(8,128)(2,1)} %bitcast.3), channel_id=1, source_target_pairs={{0,2},{1,3},{2,0},{3,1},{4,6},{5,7},{6,4},{7,5},{8,10},{9,11},{10,... | collective-permute-start | bytes 5505032 | tf_op jit(solution)/shard_map/ppermute | solution.py:19
  15.1 40.1 %copy-start = (bf16[1,3584,256]{2,1,0:T(8,128)(2,1)S(1)}, bf16[1,3584,256]{2,1,0:T(8,128)(2,1)}, u32[]{:S(2)}) copy-start(bf16[1,3584,256]{2,1,0:T(8,128)(2,1)} %param.20) | copy-start | bytes 5505028
  23.6 215.2 %collective-permute-start.3 = (bf16[256,3584]{1,0:T(8,128)(2,1)}, bf16[256,3584]{1,0:T(8,128)(2,1)}, u32[]{:S(2)}, u32[]{:S(2)}) collective-permute-start(bf16[256,3584]{1,0:T(8,128)(2,1)} %bitcast.5), channel_id=1, source_target_pairs={{0,2},{1,3},{2,0},{3,1},{4,6},{5,7},{6,4},{7,5},{8,10},{9,11},{10,... | collective-permute-start | bytes 5505032 | tf_op jit(solution)/shard_map/ppermute | solution.py:19
  55.2 185.9 %collective-permute-start.2 = (bf16[3584,256]{1,0:T(8,128)(2,1)S(1)}, bf16[3584,256]{1,0:T(8,128)(2,1)}, u32[]{:S(2)}, u32[]{:S(2)}) collective-permute-start(bf16[3584,256]{1,0:T(8,128)(2,1)S(1)} %bitcast.107), channel_id=1, source_target_pairs={{0,2},{1,3},{2,0},{3,1},{4,6},{5,7},{6,4},{7,5},{8,10},{9,11},{10,... | collective-permute-start | bytes 5505032 | tf_op jit(solution)/shard_map/ppermute | solution.py:19
  58.8 121.1 %collective-permute-start.4 = (bf16[96,3584]{1,0:T(8,128)(2,1)}, bf16[96,3584]{1,0:T(8,128)(2,1)}, u32[]{:S(2)}, u32[]{:S(2)}) collective-permute-start(bf16[96,3584]{1,0:T(8,128)(2,1)} %get-tuple-element.10), channel_id=1, source_target_pairs={{0,1},{1,0},{2,3},{3,2},{4,5},{5,4},{6,7},{7,6},{8,9},{9,8},{10,11... | collective-permute-start | bytes 2064392 | tf_op jit(solution)/shard_map/ppermute | solution.py:19
  69.8 102.2 %collective-permute-start = (bf16[96,3584]{1,0:T(8,128)(2,1)}, bf16[96,3584]{1,0:T(8,128)(2,1)}, u32[]{:S(2)}, u32[]{:S(2)}) collective-permute-start(bf16[96,3584]{1,0:T(8,128)(2,1)} %get-tuple-element.11), channel_id=1, source_target_pairs={{0,4},{1,5},{2,6},{3,7},{4,0},{5,1},{6,2},{7,3},{8,12},{9,13},{10,... | collective-permute-start | bytes 2064392 | tf_op jit(solution)/shard_map/ppermute | solution.py:14
  172.1 15.4 %collective-permute-start.14 = (bf16[96,3584]{1,0:T(8,128)(2,1)}, bf16[96,3584]{1,0:T(8,128)(2,1)}, u32[]{:S(2)}, u32[]{:S(2)}) collective-permute-start(bf16[96,3584]{1,0:T(8,128)(2,1)} %collective-permute-done.10), channel_id=1, source_target_pairs={{0,1},{1,0},{2,3},{3,2},{4,5},{5,4},{6,7},{7,6},{8,9},{9,8},{10,11... | collective-permute-start | bytes 2064392 | tf_op jit(solution)/shard_map/ppermute | solution.py:19
  179.9 22.2 %collective-permute-start.12 = (bf16[96,3584]{1,0:T(8,128)(2,1)}, bf16[96,3584]{1,0:T(8,128)(2,1)S(1)}, u32[]{:S(2)}, u32[]{:S(2)}) collective-permute-start(bf16[96,3584]{1,0:T(8,128)(2,1)} %copy-done.22), channel_id=1, source_target_pairs={{0,1},{1,0},{2,3},{3,2},{4,5},{5,4},{6,7},{7,6},{8,9},{9,8},{10,11... | collective-permute-start | bytes 2064392 | tf_op jit(solution)/shard_map/ppermute | solution.py:19
  187.5 29.4 %collective-permute-start.5 = (bf16[96,3584]{1,0:T(8,128)(2,1)}, bf16[96,3584]{1,0:T(8,128)(2,1)S(1)}, u32[]{:S(2)}, u32[]{:S(2)}) collective-permute-start(bf16[96,3584]{1,0:T(8,128)(2,1)} %collective-permute-done), channel_id=1, source_target_pairs={{0,1},{1,0},{2,3},{3,2},{4,5},{5,4},{6,7},{7,6},{8,9},{9,8},{10,11... | collective-permute-start | bytes 2064392 | tf_op jit(solution)/shard_map/ppermute | solution.py:19
  188.9 13.3 %copy-start.4 = (bf16[192,3584]{1,0:T(8,128)(2,1)S(1)}, bf16[192,3584]{1,0:T(8,128)(2,1)}, u32[]{:S(2)}) copy-start(bf16[192,3584]{1,0:T(8,128)(2,1)} %constant_dynamic-update-slice_fusion.3) | copy-start | bytes 4128772
  202.2 15.6 %copy-start.5 = (bf16[192,3584]{1,0:T(8,128)(2,1)}, bf16[192,3584]{1,0:T(8,128)(2,1)S(1)}, u32[]{:S(2)}) copy-start(bf16[192,3584]{1,0:T(8,128)(2,1)S(1)} %constant_dynamic-update-slice_fusion.2) | copy-start | bytes 4128772
  252.4 3.5 copy-start.2
  252.4 29.2 %collective-permute-start.15 = (bf16[192,3584]{1,0:T(8,128)(2,1)}, bf16[192,3584]{1,0:T(8,128)(2,1)}, u32[]{:S(2)}, u32[]{:S(2)}) collective-permute-start(bf16[192,3584]{1,0:T(8,128)(2,1)} %fusion.7), channel_id=1, source_target_pairs={{0,1},{1,0},{2,3},{3,2},{4,5},{5,4},{6,7},{7,6},{8,9},{9,8},{10,11... | collective-permute-start | bytes 4128776 | tf_op jit(solution)/shard_map/ppermute | solution.py:19
  255.9 6.5 %copy-start.9 = (bf16[96,3584]{1,0:T(8,128)(2,1)S(1)}, bf16[96,3584]{1,0:T(8,128)(2,1)}, u32[]{:S(2)}) copy-start(bf16[96,3584]{1,0:T(8,128)(2,1)} %copy-done.8) | copy-start | bytes 2064388
  261.3 49.8 %collective-permute-start.6 = (bf16[192,3584]{1,0:T(8,128)(2,1)}, bf16[192,3584]{1,0:T(8,128)(2,1)}, u32[]{:S(2)}, u32[]{:S(2)}) collective-permute-start(bf16[192,3584]{1,0:T(8,128)(2,1)} %fusion.5), channel_id=1, source_target_pairs={{0,1},{1,0},{2,3},{3,2},{4,5},{5,4},{6,7},{7,6},{8,9},{9,8},{10,11... | collective-permute-start | bytes 4128776 | tf_op jit(solution)/shard_map/ppermute | solution.py:19
  264.6 5.5 %copy-start.16 = (f32[192,256]{1,0:T(8,128)}, f32[192,256]{1,0:T(8,128)S(1)}, u32[]{:S(2)}) copy-start(f32[192,256]{1,0:T(8,128)S(1)} %fusion.148) | copy-start | bytes 589828
  288.1 23.0 %copy-start.1 = (f32[192,3584]{1,0:T(8,128)S(1)}, f32[192,3584]{1,0:T(8,128)}, u32[]{:S(2)}) copy-start(f32[192,3584]{1,0:T(8,128)} %fusion.70) | copy-start | bytes 8257540
  290.5 32.8 %collective-permute-start.16 = (bf16[96,3584]{1,0:T(8,128)(2,1)}, bf16[96,3584]{1,0:T(8,128)(2,1)}, u32[]{:S(2)}, u32[]{:S(2)}) collective-permute-start(bf16[96,3584]{1,0:T(8,128)(2,1)} %get-tuple-element.3), channel_id=1, source_target_pairs={{0,4},{1,5},{2,6},{3,7},{4,0},{5,1},{6,2},{7,3},{8,12},{9,13},{10,... | collective-permute-start | bytes 2064392 | tf_op jit(solution)/shard_map/ppermute | solution.py:14
  316.8 6.5 %copy-start.7 = (bf16[1,128,3584]{2,1,0:T(8,128)(2,1)S(1)}, bf16[1,128,3584]{2,1,0:T(8,128)(2,1)}, u32[]{:S(2)}) copy-start(bf16[1,128,3584]{2,1,0:T(8,128)(2,1)} %param.14) | copy-start | bytes 2752516
  318.2 34.4 %collective-permute-start.7 = (bf16[96,3584]{1,0:T(8,128)(2,1)S(1)}, bf16[96,3584]{1,0:T(8,128)(2,1)S(1)}, u32[]{:S(2)}, u32[]{:S(2)}) collective-permute-start(bf16[96,3584]{1,0:T(8,128)(2,1)S(1)} %get-tuple-element.9), channel_id=1, source_target_pairs={{0,4},{1,5},{2,6},{3,7},{4,0},{5,1},{6,2},{7,3},{8,12},{9,13},{10,... | collective-permute-start | bytes 2064392 | tf_op jit(solution)/shard_map/ppermute | solution.py:14
  325.1 27.6 %copy-start.13 = (bf16[1,128,3584]{2,1,0:T(8,128)(2,1)S(1)}, bf16[1,128,3584]{2,1,0:T(8,128)(2,1)}, u32[]{:S(2)}) copy-start(bf16[1,128,3584]{2,1,0:T(8,128)(2,1)} %param.11) | copy-start | bytes 2752516
  325.1 27.6 %copy-start.24 = (f32[1,128,1]{1,2,0:T(1,128)S(1)}, f32[1,128,1]{1,2,0:T(1,128)}, u32[]{:S(2)}) copy-start(f32[1,128,1]{1,2,0:T(1,128)} %param.13) | copy-start | bytes 1540
  325.7 30.4 %collective-permute-start.17 = (bf16[128,3584]{1,0:T(8,128)(2,1)S(1)}, bf16[128,3584]{1,0:T(8,128)(2,1)S(1)}, u32[]{:S(2)}, u32[]{:S(2)}) collective-permute-start(bf16[128,3584]{1,0:T(8,128)(2,1)S(1)} %fusion.14), channel_id=1, source_target_pairs={{0,24},{8,0},{16,8},{24,16},{1,25},{9,1},{17,9},{25,17},{2,26},{10... | collective-permute-start | bytes 2752520 | tf_op jit(solution)/shard_map/ppermute | solution.py:14
  353.1 13.3 %collective-permute-start.8 = (bf16[128,3584]{1,0:T(8,128)(2,1)S(1)}, bf16[128,3584]{1,0:T(8,128)(2,1)S(1)}, u32[]{:S(2)}, u32[]{:S(2)}) collective-permute-start(bf16[128,3584]{1,0:T(8,128)(2,1)S(1)} %fusion.9), channel_id=1, source_target_pairs={{0,8},{8,16},{16,24},{24,0},{1,9},{9,17},{17,25},{25,1},{2,10},{10... | collective-permute-start | bytes 2752520 | tf_op jit(solution)/shard_map/ppermute | solution.py:14
  (11 other events, 27.8 us)

commit v2 on v1

--- a/solution.py
+++ b/solution.py
@@ -1,6 +1,10 @@
+import functools
+
 import jax
 import jax.numpy as jnp
 from jax import lax
+from jax.experimental import pallas as pl
+from jax.experimental.pallas import tpu as pltpu
 from jax.sharding import PartitionSpec as P
 
 HID = 1024
@@ -87,6 +91,352 @@
         part = dot_t(gate_grad, gate) + dot_t(up_grad, up)
         total = part if total is None else total + part
     return total
+
+
+MESH = pl.DeviceIdType.MESH
+BF = jnp.bfloat16
+F32 = jnp.float32
+
+
+def slot_targets(routes, experts, capacity, mine):
+    flat = lax.rem(routes.reshape(-1) + (experts - mine), experts)
+    pairs = flat.shape[0]
+    onehot = flat[:, None] == jnp.arange(experts, dtype=jnp.int32)[None, :]
+    before = jnp.arange(pairs)[:, None] > jnp.arange(pairs)[None, :]
+    counts = dot(before.astype(BF), onehot.astype(BF))
+    ranks = jnp.sum(jnp.where(onehot, counts, 0.0), axis=1).astype(jnp.int32)
+    return flat * capacity + ranks
+
+
+def section_kernel(
+    cfg,
+    fx, bx, og, gain, fw, bw, s_f, s_b, st_f, st_b, gate, up, down,
+    next_ref, prev_ref,
+    g0, u0, g1, u1, dd, rows_f, rows_b, rows_g, out_f, out_b, out_g,
+    acc_a, acc_b, acc_c, hid, ggr, ugr, far_f, far_b, x_f, x_b, back_f, back_b,
+    ret_f, ret_b, ngr, fin_f, fin_b, tmp, scale_b,
+    w_sem, wl_sem, in_s, in_r, xl_s, xl_r, xf_s, xf_r, xo_s, xo_r, re_s, re_r, pi_s, pi_r,
+):
+    experts, group, cap, chunks, cw = cfg
+    tokens, width = fx.shape
+    rows = experts * cap
+    hd = gate.shape[1]
+    n = experts * group
+    me = lax.axis_index("expert")
+    pipe = lax.axis_index("pipe")
+    pipes = lax.axis_size("pipe")
+    xp = me + 1 - 2 * lax.rem(me, 2)
+    zp = me + 2 - 4 * lax.rem(lax.div(me, 2), 2)
+    onward = {"pipe": lax.rem(pipe + 1, pipes)}
+    behind = {"pipe": lax.rem(pipe + pipes - 1, pipes)}
+
+    def ahead_of(k):
+        return {"expert": lax.rem(me + group * k, n)}
+
+    def back_of(k):
+        return {"expert": lax.rem(me + n - group * k, n)}
+
+    def remote(src, dst, ss, rs, dev):
+        return pltpu.make_async_remote_copy(
+            src_ref=src, dst_ref=dst, send_sem=ss, recv_sem=rs, device_id=dev, device_id_type=MESH
+        )
+
+    barrier = pltpu.get_barrier_semaphore()
+    peers = [ahead_of(k) for k in range(1, experts)]
+    peers += [{"expert": xp}, {"expert": zp}, onward, behind]
+    for peer in peers:
+        pl.semaphore_signal(barrier, inc=1, device_id=peer, device_id_type=MESH)
+    pl.semaphore_wait(barrier, len(peers))
+
+    heavy = [
+        remote(src, dst, w_sem.at[0, i], w_sem.at[1, i], {"expert": zp})
+        for i, (src, dst) in enumerate(((gate, g1), (up, u1), (down, dd.at[pl.ds(hd, hd)])))
+    ]
+    local = [
+        pltpu.make_async_copy(src, dst, wl_sem.at[i])
+        for i, (src, dst) in enumerate(((gate, g0), (up, u0), (down, dd.at[pl.ds(0, hd)])))
+    ]
+
+    def col(c):
+        return pl.ds(pl.multiple_of(c * cw, cw), cw)
+
+    def each_chunk(body):
+        def step(c, carry):
+            body(c)
+            return carry
+
+        lax.fori_loop(0, chunks, step, 0)
+
+    def each_band(body):
+        def step(i, carry):
+            body(pl.ds(pl.multiple_of(i * 16, 16), 16))
+            return carry
+
+        lax.fori_loop(0, tokens // 16, step, 0)
+
+    def norm_into(src, keep):
+        def body(band):
+            wide = src[band, :].astype(F32)
+            scale = lax.rsqrt(jnp.mean(wide * wide, axis=-1, keepdims=True) + EPS)
+            tmp[band, :] = (wide * scale * gain[...]).astype(BF)
+            if keep is not None:
+                keep[band, :] = scale
+
+        each_band(body)
+
+    def weigh_into():
+        def body(band):
+            tmp[band, :] = (og[band, :].astype(F32) * bw[band, :]).astype(BF)
+
+        each_band(body)
+
+    def crossing(a, out, into):
+        return [
+            remote(
+                out.at[pl.ds((k - 1) * cap, cap)],
+                into.at[pl.ds(k * cap, cap)],
+                in_s.at[a, k - 1],
+                in_r.at[a, k - 1],
+                ahead_of(k),
+            )
+            for k in range(1, experts)
+        ]
+
+    def near_x(a, into):
+        return remote(
+            into.at[pl.ds(0, cap)], into.at[pl.ds(rows, cap)], xl_s.at[a], xl_r.at[a], {"expert": xp}
+        )
+
+    def far_x(a, into):
+        return remote(
+            into.at[pl.ds(cap, rows - cap)],
+            into.at[pl.ds(rows + cap, rows - cap)],
+            xf_s.at[a],
+            xf_r.at[a],
+            {"expert": xp},
+        )
+
+    def place(matrix, out, into):
+        def body(c):
+            picked = dot(matrix[...], tmp[:, col(c)]).astype(BF)
+            into[pl.ds(0, cap), col(c)] = picked[:cap]
+            out[:, col(c)] = picked[cap:]
+
+        each_chunk(body)
+
+    sets = ((s_f, out_f, rows_f), (s_b, out_b, rows_b), (s_b, out_g, rows_g))
+    pending = []
+    crossings, nears, fars = [], [], []
+    for a, (matrix, out, into) in enumerate(sets):
+        if a == 0:
+            norm_into(fx, None)
+        elif a == 1:
+            norm_into(bx, scale_b)
+        else:
+            weigh_into()
+        place(matrix, out, into)
+        cross = crossing(a, out, into)
+        for copy in cross:
+            copy.start()
+        near = near_x(a, into)
+        near.start()
+        crossings.append(cross)
+        nears.append(near)
+        pending += cross + [near]
+        if a == 0:
+            for copy in heavy + local:
+                copy.start()
+            pending += heavy
+
+    for a in range(3):
+        for copy in crossings[a]:
+            copy.wait_recv()
+        far = far_x(a, sets[a][2])
+        far.start()
+        fars.append(far)
+        pending.append(far)
+    for copy in local:
+        copy.wait()
+
+    def first(source, weight, acc):
+        acc[...] = jnp.zeros_like(acc)
+
+        def body(c):
+            acc[...] += dot(source[:, col(c)], weight[col(c), :])
+
+        each_chunk(body)
+
+    def first_t(source, half, acc):
+        acc[...] = jnp.zeros_like(acc)
+
+        def body(c):
+            acc[...] += dot_t(source[:, col(c)], dd[pl.ds(half * hd, hd), col(c)])
+
+        each_chunk(body)
+
+    def hidden_half(half, gw, uw):
+        first(rows_f, gw, acc_a)
+        first(rows_f, uw, acc_b)
+        pre = acc_a[...]
+        hid[:, pl.ds(half * hd, hd)] = (pre * jax.nn.sigmoid(pre) * acc_b[...]).astype(BF)
+
+    def grads_half(half, gw, uw):
+        first(rows_b, gw, acc_a)
+        first(rows_b, uw, acc_b)
+        first_t(rows_g, half, acc_c)
+        pre, upb, hg = acc_a[...], acc_b[...], acc_c[...]
+        sig = jax.nn.sigmoid(pre)
+        ggr[:, pl.ds(half * hd, hd)] = (hg * upb * sig * (1.0 + pre * (1.0 - sig))).astype(BF)
+        ugr[:, pl.ds(half * hd, hd)] = (hg * pre * sig).astype(BF)
+
+    nears[0].wait_recv()
+    fars[0].wait_recv()
+    hidden_half(0, g0, u0)
+    for a in (1, 2):
+        nears[a].wait_recv()
+        fars[a].wait_recv()
+    grads_half(0, g0, u0)
+    for copy in heavy:
+        copy.wait_recv()
+    hidden_half(1, g1, u1)
+
+    def sum_f(at, c):
+        return dot(hid[pl.ds(at, rows), :], dd[:, col(c)])
+
+    def sum_b(at, c):
+        ga, ua = ggr[pl.ds(at, rows), :], ugr[pl.ds(at, rows), :]
+        total = dot_t(ga[:, :hd], g0[col(c), :]) + dot_t(ga[:, hd:], g1[col(c), :])
+        return total + dot_t(ua[:, :hd], u0[col(c), :]) + dot_t(ua[:, hd:], u1[col(c), :])
+
+    def x_out(a, c):
+        src, dst = ((far_f, x_f), (far_b, x_b))[a]
+        return remote(src.at[c], dst.at[c], xo_s.at[a, c], xo_r.at[a, c], {"expert": xp})
+
+    def going_back(a, c):
+        src, dst = ((ret_f, back_f), (ret_b, back_b))[a]
+        return [
+            remote(
+                src.at[c, pl.ds((k - 1) * cap, cap)],
+                dst.at[c, pl.ds(k * cap, cap)],
+                re_s.at[a, c, k - 1],
+                re_r.at[a, c, k - 1],
+                back_of(k),
+            )
+            for k in range(1, experts)
+        ]
+
+    def leaving(a, c):
+        src, dst, dev = ((fin_f, next_ref, onward), (fin_b, prev_ref, behind))[a]
+        return remote(src.at[c], dst.at[:, col(c)], pi_s.at[a, c], pi_r.at[a, c], dev)
+
+    def far_step_f(c):
+        far_f[c] = sum_f(rows, c).astype(BF)
+        x_out(0, c).start()
+
+    each_chunk(far_step_f)
+    grads_half(1, g1, u1)
+
+    def far_step_b(c):
+        far_b[c] = sum_b(rows, c).astype(BF)
+
+    each_chunk(far_step_b)
+
+    def near_step(a, summed, x_in, back, ret):
+        def body(c):
+            total = summed(0, c)
+            x_out(a, c).wait_recv()
+            total = (total + x_in[c].astype(F32)).astype(BF)
+            back[c, pl.ds(0, cap), :] = total[:cap]
+            ret[c] = total[cap:]
+            for copy in going_back(a, c):
+                copy.start()
+
+        return body
+
+    each_chunk(near_step(0, sum_f, x_f, back_f, ret_f))
+
+    def start_b(c):
+        x_out(1, c).start()
+
+    each_chunk(start_b)
+    each_chunk(near_step(1, sum_b, x_b, back_b, ret_b))
+
+    def final_f(c):
+        for copy in going_back(0, c):
+            copy.wait_recv()
+        values = dot(st_f[...], back_f[c])
+        fin_f[c] = (fx[:, col(c)].astype(F32) + fw[...] * values).astype(BF)
+        leaving(0, c).start()
+
+    each_chunk(final_f)
+
+    def gather_b(c, carry):
+        for copy in going_back(1, c):
+            copy.wait_recv()
+        unit_grad = gain[:, col(c)] * dot(st_b[...], back_b[c])
+        ngr[c] = unit_grad
+        unit = bx[:, col(c)].astype(F32) * scale_b[...]
+        return carry + jnp.sum(unit_grad * unit, axis=-1, keepdims=True)
+
+    mean = lax.fori_loop(0, chunks, gather_b, jnp.zeros((tokens, 1), F32)) / width
+
+    def final_b(c):
+        unit = bx[:, col(c)].astype(F32) * scale_b[...]
+        grad = og[:, col(c)].astype(F32) + scale_b[...] * (ngr[c] - unit * mean)
+        fin_b[c] = grad.astype(BF)
+        leaving(1, c).start()
+
+    each_chunk(final_b)
+
+    for copy in pending:
+        copy.wait_send()
+
+    def drain(c):
+        for a in range(2):
+            x_out(a, c).wait_send()
+            for copy in going_back(a, c):
+                copy.wait_send()
+            leaving(a, c).wait()
+
+    each_chunk(drain)
+
+
+def fused(fi, fr, fwt, bi, br, bwt, og, gain, gate, up, down, experts, group, cap):
+    tokens, width = fi.shape
+    hd = gate.shape[1]
+    rows = experts * cap
+    cw = 512
+    chunks = width // cw
+    mine = lax.axis_index("expert") // group
+    slots = jnp.arange(rows, dtype=jnp.int32)
+    t_f = slot_targets(fr, experts, cap, mine)
+    t_b = slot_targets(br, experts, cap, mine)
+    s_f, s_b = [(slots[:, None] == t[None, :]).astype(BF) for t in (t_f, t_b)]
+    st_f, st_b = [(t[:, None] == slots[None, :]).astype(BF) for t in (t_f, t_b)]
+    vm = pltpu.VMEM
+    sem = pltpu.SemaphoreType.DMA
+    others = experts - 1
+    scratch = [vm((width, hd), BF)] * 4 + [vm((2 * hd, width), BF)]
+    scratch += [vm((2 * rows, width), BF)] * 3 + [vm((others * cap, width), BF)] * 3
+    scratch += [vm((2 * rows, hd), F32)] * 3 + [vm((2 * rows, 2 * hd), BF)] * 3
+    scratch += [vm((chunks, rows, cw), BF)] * 6 + [vm((chunks, others * cap, cw), BF)] * 2
+    scratch += [vm((chunks, tokens, cw), F32)] + [vm((chunks, tokens, cw), BF)] * 2
+    scratch += [vm((tokens, width), BF), vm((tokens, 1), F32)]
+    scratch += [sem((2, 3)), sem((3,)), sem((3, others)), sem((3, others))]
+    scratch += [sem((3,))] * 4 + [sem((2, chunks))] * 2
+    scratch += [sem((2, chunks, others))] * 2 + [sem((2, chunks))] * 2
+    out = jax.ShapeDtypeStruct((tokens, width), BF)
+    anywhere = pl.BlockSpec(memory_space=pl.ANY)
+    return pl.pallas_call(
+        functools.partial(section_kernel, (experts, group, cap, chunks, cw)),
+        out_shape=(out, out),
+        in_specs=[pl.BlockSpec(memory_space=vm)] * 10 + [anywhere] * 3,
+        out_specs=(anywhere, anywhere),
+        scratch_shapes=scratch,
+        compiler_params=pltpu.CompilerParams(
+            collective_id=0, has_side_effects=True, vmem_limit_bytes=58 * 1024 * 1024
+        ),
+    )(fi, bi, og, gain, fwt, bwt, s_f, s_b, st_f, st_b, gate, up, down)
 
 
 def per_device(
@@ -109,6 +459,14 @@
     top = forward_route.shape[2]
     width = forward_input.shape[2]
     capacity = max(2, 3 * tokens * top // (2 * experts))
+    if top == 1 and capacity % 16 == 0 and tokens % 16 == 0 and width % 512 == 0:
+        next_input, previous_grad = fused(
+            forward_input[0], forward_route[0], forward_weight[0],
+            backward_input[0], backward_route[0], backward_weight[0],
+            output_grad[0], norm_gain, gate_weight[0], up_weight[0], down_weight[0],
+            experts, group, capacity,
+        )
+        return (next_input[None], previous_grad[None])
     mine = lax.axis_index("expert") // group
     gain = norm_gain[0]
     own = (gate_weight[0], up_weight[0], down_weight[0])

time: 370 us -> 291 us (0.79)
  Pallas kernels: 0 us -> 275 us
  waiting for transfers between devices: 214 us -> 0 us
  matrix products: 94.8 us -> 0.3 us
  starting transfers between devices: 40.1 us -> 0 us
  local copies, waits for them, and re-layouts: 13.7 us -> 5.95 us
    pallas_call x0 -> x1, Pallas kernels: none -> 275 us  [fused(): pl.pallas_call(functools.partial(section_kernel, (experts, group, cap, ch...]
    ppermute x18 -> x0, waiting for transfers between devices: 214 us -> none  [the longest x7 150 us: passed_along(): lax.ppermute(array, axis, [(i, (i + by) % devices) for i in range(devices)])]
    dot_general x19 -> x0, matrix products: 52.3 us -> none  [the longest x12 46.7 us: dot_t(): lax.dot_general(a, b, (((1,), (1,)), ((), ())), preferred_element_type=jn...]
    dot_general x12 -> x2, matrix products: 42.5 us -> 0.3 us  [dot(): return jnp.dot(a, b, preferred_element_type=jnp.float32)]
    ppermute x18 -> x0, starting transfers between devices: 40.1 us -> none  [the longest x7 30.4 us: passed_along(): lax.ppermute(array, axis, [(i, (i + by) % devices) for i in range(devices)])]
    split x5 -> x0, local copies, waits for them, and re-layouts: 5.21 us -> none  [across(): blocks = jnp.split(slots, experts, axis=0)]
  transfers between devices with their start and end apart: 18 -> 0, of which waited for: 12 -> 0; matrix products, arithmetic and copies ran while one was open for 25% -> 0% of each run, Pallas kernels for 0% -> 0%
where the time goes in v2:
time: 291 us; the launch traced here: 286 us
  Pallas kernels  275 us (95%)
  local copies, waits for them, and re-layouts  5.95 us (2%)
  other arithmetic  3.4 us (1%)
    pallas_call x1, Pallas kernels, fused(): pl.pallas_call(functools.partial(section_kernel, (experts, group, cap, ch...  275 us

profile of v2, /device:TPU:1, one launch (start us, length us, event | category | flops | bytes accessed | tf_op | source)
XLA Modules:
  0.0 285.6 jit_solution(655569650195512675)
XLA Ops:
  0.6 0.7 compare_select_fusion
  1.3 0.1 fusion.1
  1.5 0.2 fusion
  1.7 0.6 fusion.4.s_f
  2.3 0.6 fusion.5.s_b
  3.0 0.7 fusion.3.st_b
  3.7 0.7 fusion.2.st_f
  4.4 1.4 copy.13.fw
  5.8 1.4 copy.14.bw
  7.1 275.3 %shard_map.122 = (bf16[128,3584]{1,0:T(8,128)(2,1)}, bf16[128,3584]{1,0:T(8,128)(2,1)}) custom-call(bf16[128,3584]{1,0:T(8,128)(2,1)} %bitcast.17, bf16[128,3584]{1,0:T(8,128)(2,1)} %bitcast.18, bf16[128,3584]{1,0:T(8,128)(2,1)} %bitcast.19, f32[1,3584]{1,0:T(1,128)} %gain.1, f32[128,1]{1,0:T(8,128)} %copy.13.fw, f32[128,1]{1,0:T(8,128)} %copy.14.bw, ...), custom_call_target="tpu_custom_call" | custom-call | tf_op jit(solution)/shard_map/pallas_call | solution.py:430
  282.4 0.0 copy-start
  282.4 2.2 copy.17
  284.7 0.0 copy-done
  284.7 0.9 copy.18
  (2 shorter events, 0.0 us)
Async XLA Ops:
  282.4 2.3 copy-start

commit v3 on v2

--- a/solution.py
+++ b/solution.py
@@ -98,24 +98,32 @@
 F32 = jnp.float32
 
 
-def slot_targets(routes, experts, capacity, mine):
-    flat = lax.rem(routes.reshape(-1) + (experts - mine), experts)
-    pairs = flat.shape[0]
-    onehot = flat[:, None] == jnp.arange(experts, dtype=jnp.int32)[None, :]
-    before = jnp.arange(pairs)[:, None] > jnp.arange(pairs)[None, :]
-    counts = dot(before.astype(BF), onehot.astype(BF))
-    ranks = jnp.sum(jnp.where(onehot, counts, 0.0), axis=1).astype(jnp.int32)
-    return flat * capacity + ranks
+def slot_masks(col, row, experts, cap, mine):
+    def relative(route):
+        return jnp.where(route >= mine, route - mine, route - mine + experts).astype(F32)
+
+    tokens, rows = col.shape[0], experts * cap
+    rel_c, rel_r = relative(col), relative(row)
+    first = lax.broadcasted_iota(jnp.int32, (tokens, tokens), 0)
+    second = lax.broadcasted_iota(jnp.int32, (tokens, tokens), 1)
+    same = jnp.where(rel_c == rel_r, 1.0, 0.0)
+    rank_c = jnp.sum(jnp.where(first > second, same, 0.0), axis=1, keepdims=True)
+    rank_r = jnp.sum(jnp.where(first < second, same, 0.0), axis=0, keepdims=True)
+    down = lax.broadcasted_iota(jnp.int32, (rows, tokens), 0).astype(F32)
+    along = lax.broadcasted_iota(jnp.int32, (tokens, rows), 1).astype(F32)
+    to_slot = jnp.where(down == rel_r * cap + rank_r, 1.0, 0.0).astype(BF)
+    from_slot = jnp.where(along == rel_c * cap + rank_c, 1.0, 0.0).astype(BF)
+    return to_slot, from_slot
 
 
 def section_kernel(
     cfg,
-    fx, bx, og, gain, fw, bw, s_f, s_b, st_f, st_b, gate, up, down,
+    fx, bx, og, gain, fw, bw, fr_c, fr_r, br_c, br_r, gate, up, down,
     next_ref, prev_ref,
     g0, u0, g1, u1, dd, rows_f, rows_b, rows_g, out_f, out_b, out_g,
     acc_a, acc_b, acc_c, hid, ggr, ugr, far_f, far_b, x_f, x_b, back_f, back_b,
-    ret_f, ret_b, ngr, fin_f, fin_b, tmp, scale_b,
-    w_sem, wl_sem, in_s, in_r, xl_s, xl_r, xf_s, xf_r, xo_s, xo_r, re_s, re_r, pi_s, pi_r,
+    ret_f, ret_b, ngr, fin_f, fin_b, tmp, scale_b, s_f, s_b, st_f, st_b,
+    w_sem, d_s, d_r, wl_sem, in_s, in_r, xl_s, xl_r, xf_s, xf_r, xo_s, xo_r, re_s, re_r, pi_s, pi_r,
 ):
     experts, group, cap, chunks, cw = cfg
     tokens, width = fx.shape
@@ -150,13 +158,18 @@
 
     heavy = [
         remote(src, dst, w_sem.at[0, i], w_sem.at[1, i], {"expert": zp})
-        for i, (src, dst) in enumerate(((gate, g1), (up, u1), (down, dd.at[pl.ds(hd, hd)])))
+        for i, (src, dst) in enumerate(((gate, g1), (up, u1)))
     ]
+    for copy in heavy:
+        copy.start()
     local = [
         pltpu.make_async_copy(src, dst, wl_sem.at[i])
         for i, (src, dst) in enumerate(((gate, g0), (up, u0), (down, dd.at[pl.ds(0, hd)])))
     ]
 
+    for copy in local:
+        copy.start()
+
     def col(c):
         return pl.ds(pl.multiple_of(c * cw, cw), cw)
 
@@ -166,6 +179,11 @@
             return carry
 
         lax.fori_loop(0, chunks, step, 0)
+
+    def down_chunk(c):
+        return remote(
+            down.at[:, col(c)], dd.at[pl.ds(hd, hd), col(c)], d_s.at[c], d_r.at[c], {"expert": zp}
+        )
 
     def each_band(body):
         def step(i, carry):
@@ -224,6 +242,9 @@
 
         each_chunk(body)
 
+    mine = lax.div(me, group)
+    s_f[...], st_f[...] = slot_masks(fr_c[...], fr_r[...], experts, cap, mine)
+    s_b[...], st_b[...] = slot_masks(br_c[...], br_r[...], experts, cap, mine)
     sets = ((s_f, out_f, rows_f), (s_b, out_b, rows_b), (s_b, out_g, rows_g))
     pending = []
     crossings, nears, fars = [], [], []
@@ -243,10 +264,6 @@
         crossings.append(cross)
         nears.append(near)
         pending += cross + [near]
-        if a == 0:
-            for copy in heavy + local:
-                copy.start()
-            pending += heavy
 
     for a in range(3):
         for copy in crossings[a]:
@@ -255,6 +272,13 @@
         far.start()
         fars.append(far)
         pending.append(far)
+    for copy in heavy:
+        copy.wait_send()
+
+    def start_down(c):
+        down_chunk(c).start()
+
+    each_chunk(start_down)
     for copy in local:
         copy.wait()
 
@@ -266,13 +290,8 @@
 
         each_chunk(body)
 
-    def first_t(source, half, acc):
-        acc[...] = jnp.zeros_like(acc)
-
-        def body(c):
-            acc[...] += dot_t(source[:, col(c)], dd[pl.ds(half * hd, hd), col(c)])
-
-        each_chunk(body)
+    def add_t(half, c):
+        acc_c[...] += dot_t(rows_g[:, col(c)], dd[pl.ds(half * hd, hd), col(c)])
 
     def hidden_half(half, gw, uw):
         first(rows_f, gw, acc_a)
@@ -280,10 +299,12 @@
         pre = acc_a[...]
         hid[:, pl.ds(half * hd, hd)] = (pre * jax.nn.sigmoid(pre) * acc_b[...]).astype(BF)
 
-    def grads_half(half, gw, uw):
+    def grads_start(gw, uw):
         first(rows_b, gw, acc_a)
         first(rows_b, uw, acc_b)
-        first_t(rows_g, half, acc_c)
+        acc_c[...] = jnp.zeros_like(acc_c)
+
+    def grads_end(half):
         pre, upb, hg = acc_a[...], acc_b[...], acc_c[...]
         sig = jax.nn.sigmoid(pre)
         ggr[:, pl.ds(half * hd, hd)] = (hg * upb * sig * (1.0 + pre * (1.0 - sig))).astype(BF)
@@ -295,10 +316,13 @@
     for a in (1, 2):
         nears[a].wait_recv()
         fars[a].wait_recv()
-    grads_half(0, g0, u0)
+    grads_start(g0, u0)
+    each_chunk(functools.partial(add_t, 0))
+    grads_end(0)
     for copy in heavy:
         copy.wait_recv()
     hidden_half(1, g1, u1)
+    grads_start(g1, u1)
 
     def sum_f(at, c):
         return dot(hid[pl.ds(at, rows), :], dd[:, col(c)])
@@ -330,14 +354,17 @@
         return remote(src.at[c], dst.at[:, col(c)], pi_s.at[a, c], pi_r.at[a, c], dev)
 
     def far_step_f(c):
+        down_chunk(c).wait_recv()
         far_f[c] = sum_f(rows, c).astype(BF)
         x_out(0, c).start()
+        add_t(1, c)
 
     each_chunk(far_step_f)
-    grads_half(1, g1, u1)
+    grads_end(1)
 
     def far_step_b(c):
         far_b[c] = sum_b(rows, c).astype(BF)
+        x_out(1, c).start()
 
     each_chunk(far_step_b)
 
@@ -354,12 +381,7 @@
         return body
 
     each_chunk(near_step(0, sum_f, x_f, back_f, ret_f))
-
-    def start_b(c):
-        x_out(1, c).start()
-
-    each_chunk(start_b)
-    each_chunk(near_step(1, sum_b, x_b, back_b, ret_b))
+    near_b = near_step(1, sum_b, x_b, back_b, ret_b)
 
     def final_f(c):
         for copy in going_back(0, c):
@@ -368,7 +390,11 @@
         fin_f[c] = (fx[:, col(c)].astype(F32) + fw[...] * values).astype(BF)
         leaving(0, c).start()
 
-    each_chunk(final_f)
+    def near_b_final_f(c):
+        near_b(c)
+        final_f(c)
+
+    each_chunk(near_b_final_f)
 
     def gather_b(c, carry):
         for copy in going_back(1, c):
@@ -392,6 +418,7 @@
         copy.wait_send()
 
     def drain(c):
+        down_chunk(c).wait_send()
         for a in range(2):
             x_out(a, c).wait_send()
             for copy in going_back(a, c):
@@ -407,12 +434,6 @@
     rows = experts * cap
     cw = 512
     chunks = width // cw
-    mine = lax.axis_index("expert") // group
-    slots = jnp.arange(rows, dtype=jnp.int32)
-    t_f = slot_targets(fr, experts, cap, mine)
-    t_b = slot_targets(br, experts, cap, mine)
-    s_f, s_b = [(slots[:, None] == t[None, :]).astype(BF) for t in (t_f, t_b)]
-    st_f, st_b = [(t[:, None] == slots[None, :]).astype(BF) for t in (t_f, t_b)]
     vm = pltpu.VMEM
     sem = pltpu.SemaphoreType.DMA
     others = experts - 1
@@ -422,7 +443,8 @@
     scratch += [vm((chunks, rows, cw), BF)] * 6 + [vm((chunks, others * cap, cw), BF)] * 2
     scratch += [vm((chunks, tokens, cw), F32)] + [vm((chunks, tokens, cw), BF)] * 2
     scratch += [vm((tokens, width), BF), vm((tokens, 1), F32)]
-    scratch += [sem((2, 3)), sem((3,)), sem((3, others)), sem((3, others))]
+    scratch += [vm((rows, tokens), BF)] * 2 + [vm((tokens, rows), BF)] * 2
+    scratch += [sem((2, 2)), sem((chunks,)), sem((chunks,)), sem((3,)), sem((3, others)), sem((3, others))]
     scratch += [sem((3,))] * 4 + [sem((2, chunks))] * 2
     scratch += [sem((2, chunks, others))] * 2 + [sem((2, chunks))] * 2
     out = jax.ShapeDtypeStruct((tokens, width), BF)
@@ -436,7 +458,7 @@
         compiler_params=pltpu.CompilerParams(
             collective_id=0, has_side_effects=True, vmem_limit_bytes=58 * 1024 * 1024
         ),
-    )(fi, bi, og, gain, fwt, bwt, s_f, s_b, st_f, st_b, gate, up, down)
+    )(fi, bi, og, gain, fwt, bwt, fr, fr.T, br, br.T, gate, up, down)
 
 
 def per_device(

time: 291 us -> 258 us (0.89); the launches traced: 286 us -> 258 us
  Pallas kernels: 275 us -> 248 us
  other arithmetic: 3.4 us -> 0 us
    pallas_call x1, Pallas kernels: 275 us -> 248 us  [fused(): pl.pallas_call(functools.partial(section_kernel, (experts, group, cap, ch...]
where the time goes in v3:
time: 258 us
  Pallas kernels  248 us (96%)
  local copies, waits for them, and re-layouts  8.69 us (3%)
    pallas_call x1, Pallas kernels, fused(): pl.pallas_call(functools.partial(section_kernel, (experts, group, cap, ch...  248 us

profile of v3, /device:TPU:1, one launch (start us, length us, event | category | flops | bytes accessed | tf_op | source)
XLA Modules:
  0.0 257.8 jit_solution(1385570145067608073)
XLA Ops:
  0.6 1.4 copy.13.fw
  2.0 1.4 copy.14.bw
  3.4 1.4 copy.16.br_c
  4.8 1.4 copy.15.fr_c
  6.2 248.5 %shard_map.122 = (bf16[128,3584]{1,0:T(8,128)(2,1)}, bf16[128,3584]{1,0:T(8,128)(2,1)}) custom-call(bf16[128,3584]{1,0:T(8,128)(2,1)} %bitcast.19, bf16[128,3584]{1,0:T(8,128)(2,1)} %bitcast.20, bf16[128,3584]{1,0:T(8,128)(2,1)} %bitcast.21, f32[1,3584]{1,0:T(1,128)} %gain.1, f32[128,1]{1,0:T(8,128)} %copy.13.fw, f32[128,1]{1,0:T(8,128)} %copy.14.bw, ...), custom_call_target="tpu_custom_call" | custom-call | tf_op jit(solution)/shard_map/pallas_call | solution.py:452
  254.6 0.0 copy-start
  254.6 2.2 copy.19
  256.9 0.0 copy-done
  256.9 0.9 copy.20
Async XLA Ops:
  254.6 2.3 copy-start

commit v4 on v3

--- a/solution.py
+++ b/solution.py
@@ -122,7 +122,7 @@
     next_ref, prev_ref,
     g0, u0, g1, u1, dd, rows_f, rows_b, rows_g, out_f, out_b, out_g,
     acc_a, acc_b, acc_c, hid, ggr, ugr, far_f, far_b, x_f, x_b, back_f, back_b,
-    ret_f, ret_b, ngr, fin_f, fin_b, tmp, scale_b, s_f, s_b, st_f, st_b,
+    ret_f, ret_b, ngr, fin_f, fin_b, tmp, scale_b, s_f, s_b, st_f, st_b, sum_f, sum_b,
     w_sem, d_s, d_r, wl_sem, in_s, in_r, xl_s, xl_r, xf_s, xf_r, xo_s, xo_r, re_s, re_r, pi_s, pi_r,
 ):
     experts, group, cap, chunks, cw = cfg
@@ -313,24 +313,27 @@
     nears[0].wait_recv()
     fars[0].wait_recv()
     hidden_half(0, g0, u0)
+
+    def own_f(c):
+        sum_f[c] = dot(hid[:, pl.ds(0, hd)], dd[pl.ds(0, hd), col(c)])
+
+    each_chunk(own_f)
     for a in (1, 2):
         nears[a].wait_recv()
         fars[a].wait_recv()
     grads_start(g0, u0)
     each_chunk(functools.partial(add_t, 0))
     grads_end(0)
+
+    def own_b(c):
+        part = dot_t(ggr[:, pl.ds(0, hd)], g0[col(c), :])
+        sum_b[c] = part + dot_t(ugr[:, pl.ds(0, hd)], u0[col(c), :])
+
+    each_chunk(own_b)
     for copy in heavy:
         copy.wait_recv()
     hidden_half(1, g1, u1)
     grads_start(g1, u1)
-
-    def sum_f(at, c):
-        return dot(hid[pl.ds(at, rows), :], dd[:, col(c)])
-
-    def sum_b(at, c):
-        ga, ua = ggr[pl.ds(at, rows), :], ugr[pl.ds(at, rows), :]
-        total = dot_t(ga[:, :hd], g0[col(c), :]) + dot_t(ga[:, hd:], g1[col(c), :])
-        return total + dot_t(ua[:, :hd], u0[col(c), :]) + dot_t(ua[:, hd:], u1[col(c), :])
 
     def x_out(a, c):
         src, dst = ((far_f, x_f), (far_b, x_b))[a]
@@ -355,24 +358,28 @@
 
     def far_step_f(c):
         down_chunk(c).wait_recv()
-        far_f[c] = sum_f(rows, c).astype(BF)
+        total = sum_f[c] + dot(hid[:, pl.ds(hd, hd)], dd[pl.ds(hd, hd), col(c)])
+        far_f[c] = total[rows:].astype(BF)
         x_out(0, c).start()
+        sum_f[c, pl.ds(0, rows), :] = total[:rows]
         add_t(1, c)
 
     each_chunk(far_step_f)
     grads_end(1)
 
     def far_step_b(c):
-        far_b[c] = sum_b(rows, c).astype(BF)
+        total = sum_b[c] + dot_t(ggr[:, pl.ds(hd, hd)], g1[col(c), :])
+        total = total + dot_t(ugr[:, pl.ds(hd, hd)], u1[col(c), :])
+        far_b[c] = total[rows:].astype(BF)
         x_out(1, c).start()
+        sum_b[c, pl.ds(0, rows), :] = total[:rows]
 
     each_chunk(far_step_b)
 
     def near_step(a, summed, x_in, back, ret):
         def body(c):
-            total = summed(0, c)
             x_out(a, c).wait_recv()
-            total = (total + x_in[c].astype(F32)).astype(BF)
+            total = (summed[c, pl.ds(0, rows), :] + x_in[c].astype(F32)).astype(BF)
             back[c, pl.ds(0, cap), :] = total[:cap]
             ret[c] = total[cap:]
             for copy in going_back(a, c):
@@ -444,6 +451,7 @@
     scratch += [vm((chunks, tokens, cw), F32)] + [vm((chunks, tokens, cw), BF)] * 2
     scratch += [vm((tokens, width), BF), vm((tokens, 1), F32)]
     scratch += [vm((rows, tokens), BF)] * 2 + [vm((tokens, rows), BF)] * 2
+    scratch += [vm((chunks, 2 * rows, cw), F32)] * 2
     scratch += [sem((2, 2)), sem((chunks,)), sem((chunks,)), sem((3,)), sem((3, others)), sem((3, others))]
     scratch += [sem((3,))] * 4 + [sem((2, chunks))] * 2
     scratch += [sem((2, chunks, others))] * 2 + [sem((2, chunks))] * 2

time: 258 us -> 257 us (level)
  no operation moved by 1% of the time
where the time goes in v4:
time: 257 us
  Pallas kernels  248 us (96%)
  local copies, waits for them, and re-layouts  8.69 us (3%)
    pallas_call x1, Pallas kernels, fused(): pl.pallas_call(functools.partial(section_kernel, (experts, group, cap, ch...  248 us

profile of v4, /device:TPU:1, one launch (start us, length us, event | category | flops | bytes accessed | tf_op | source)
XLA Modules:
  0.0 257.2 jit_solution(16836234140784263374)
XLA Ops:
  0.6 1.4 copy.13.fw
  2.0 1.4 copy.14.bw
  3.4 1.4 copy.16.br_c
  4.8 1.4 copy.15.fr_c
  6.2 247.8 %shard_map.122 = (bf16[128,3584]{1,0:T(8,128)(2,1)}, bf16[128,3584]{1,0:T(8,128)(2,1)}) custom-call(bf16[128,3584]{1,0:T(8,128)(2,1)} %bitcast.19, bf16[128,3584]{1,0:T(8,128)(2,1)} %bitcast.20, bf16[128,3584]{1,0:T(8,128)(2,1)} %bitcast.21, f32[1,3584]{1,0:T(1,128)} %gain.1, f32[128,1]{1,0:T(8,128)} %copy.13.fw, f32[128,1]{1,0:T(8,128)} %copy.14.bw, ...), custom_call_target="tpu_custom_call" | custom-call | tf_op jit(solution)/shard_map/pallas_call | solution.py:460
  254.0 0.0 copy-start
  254.0 2.2 copy.19
  256.3 0.0 copy-done
  256.3 0.9 copy.20
Async XLA Ops:
  254.0 2.3 copy-start

commit v5 on v4

--- a/solution.py
+++ b/solution.py
@@ -98,14 +98,19 @@
 F32 = jnp.float32
 
 
-def slot_masks(col, row, experts, cap, mine):
+def slot_masks(row, scale_row, experts, cap, mine):
     def relative(route):
         return jnp.where(route >= mine, route - mine, route - mine + experts).astype(F32)
 
-    tokens, rows = col.shape[0], experts * cap
-    rel_c, rel_r = relative(col), relative(row)
+    tokens, rows = row.shape[1], experts * cap
+    rel_r = relative(row)
     first = lax.broadcasted_iota(jnp.int32, (tokens, tokens), 0)
     second = lax.broadcasted_iota(jnp.int32, (tokens, tokens), 1)
+
+    def upright(values):
+        return jnp.sum(jnp.where(first == second, values, 0.0), axis=1, keepdims=True)
+
+    rel_c = upright(rel_r)
     same = jnp.where(rel_c == rel_r, 1.0, 0.0)
     rank_c = jnp.sum(jnp.where(first > second, same, 0.0), axis=1, keepdims=True)
     rank_r = jnp.sum(jnp.where(first < second, same, 0.0), axis=0, keepdims=True)
@@ -113,17 +118,17 @@
     along = lax.broadcasted_iota(jnp.int32, (tokens, rows), 1).astype(F32)
     to_slot = jnp.where(down == rel_r * cap + rank_r, 1.0, 0.0).astype(BF)
     from_slot = jnp.where(along == rel_c * cap + rank_c, 1.0, 0.0).astype(BF)
-    return to_slot, from_slot
+    return to_slot, from_slot, upright(scale_row)
 
 
 def section_kernel(
     cfg,
-    fx, bx, og, gain, fw, bw, fr_c, fr_r, br_c, br_r, gate, up, down,
+    fx, bx, og, gain, fw_r, bw_r, fr_r, br_r, gate, up, down,
     next_ref, prev_ref,
     g0, u0, g1, u1, dd, rows_f, rows_b, rows_g, out_f, out_b, out_g,
     acc_a, acc_b, acc_c, hid, ggr, ugr, far_f, far_b, x_f, x_b, back_f, back_b,
-    ret_f, ret_b, ngr, fin_f, fin_b, tmp, scale_b, s_f, s_b, st_f, st_b, sum_f, sum_b,
-    w_sem, d_s, d_r, wl_sem, in_s, in_r, xl_s, xl_r, xf_s, xf_r, xo_s, xo_r, re_s, re_r, pi_s, pi_r,
+    ret_f, ret_b, ngr, fin_f, fin_b, tmp, scale_b, s_f, s_b, st_f, st_b, sum_f, sum_b, fw, bw,
+    w_s, w_r, d_s, d_r, wl_sem, in_s, in_r, xl_s, xl_r, xf_s, xf_r, xo_s, xo_r, re_s, re_r, pi_s, pi_r,
 ):
     experts, group, cap, chunks, cw = cfg
     tokens, width = fx.shape
@@ -156,20 +161,11 @@
         pl.semaphore_signal(barrier, inc=1, device_id=peer, device_id_type=MESH)
     pl.semaphore_wait(barrier, len(peers))
 
-    heavy = [
-        remote(src, dst, w_sem.at[0, i], w_sem.at[1, i], {"expert": zp})
-        for i, (src, dst) in enumerate(((gate, g1), (up, u1)))
-    ]
-    for copy in heavy:
-        copy.start()
     local = [
         pltpu.make_async_copy(src, dst, wl_sem.at[i])
         for i, (src, dst) in enumerate(((gate, g0), (up, u0), (down, dd.at[pl.ds(0, hd)])))
     ]
 
-    for copy in local:
-        copy.start()
-
     def col(c):
         return pl.ds(pl.multiple_of(c * cw, cw), cw)
 
@@ -180,10 +176,28 @@
 
         lax.fori_loop(0, chunks, step, 0)
 
+    def thick_chunk(kind, c):
+        src, dst = ((gate, g1), (up, u1))[kind]
+        return remote(
+            src.at[col(c)], dst.at[col(c)], w_s.at[kind, c], w_r.at[kind, c], {"expert": zp}
+        )
+
     def down_chunk(c):
         return remote(
             down.at[:, col(c)], dd.at[pl.ds(hd, hd), col(c)], d_s.at[c], d_r.at[c], {"expert": zp}
         )
+
+    thick = [(kind, c) for c in range(chunks) for kind in range(2)]
+
+    def send_weights(count):
+        for kind, c in thick[:count]:
+            thick_chunk(kind, c).start()
+        del thick[:count]
+
+    send_weights(2)
+    for copy in local:
+        copy.start()
+    send_weights(1)
 
     def each_band(body):
         def step(i, carry):
@@ -208,31 +222,36 @@
 
         each_band(body)
 
+    half = cap // 2
+
     def crossing(a, out, into):
         return [
             remote(
-                out.at[pl.ds((k - 1) * cap, cap)],
-                into.at[pl.ds(k * cap, cap)],
-                in_s.at[a, k - 1],
-                in_r.at[a, k - 1],
+                out.at[pl.ds((k - 1) * cap + i * half, half)],
+                into.at[pl.ds(k * cap + i * half, half)],
+                in_s.at[a, k - 1, i],
+                in_r.at[a, k - 1, i],
                 ahead_of(k),
             )
+            for i in range(2)
             for k in range(1, experts)
         ]
 
-    def near_x(a, into):
+    def to_x(a, into, start, size, i, ss, rs):
         return remote(
-            into.at[pl.ds(0, cap)], into.at[pl.ds(rows, cap)], xl_s.at[a], xl_r.at[a], {"expert": xp}
-        )
-
-    def far_x(a, into):
-        return remote(
-            into.at[pl.ds(cap, rows - cap)],
-            into.at[pl.ds(rows + cap, rows - cap)],
-            xf_s.at[a],
-            xf_r.at[a],
+            into.at[pl.ds(start, size)],
+            into.at[pl.ds(rows + start, size)],
+            ss.at[a, i],
+            rs.at[a, i],
             {"expert": xp},
         )
+
+    def near_x(a, into):
+        return [to_x(a, into, i * half, half, i, xl_s, xl_r) for i in range(2)]
+
+    def far_x(a, into):
+        size = (rows - cap) // 2
+        return [to_x(a, into, cap + i * size, size, i, xf_s, xf_r) for i in range(2)]
 
     def place(matrix, out, into):
         def body(c):
@@ -243,8 +262,8 @@
         each_chunk(body)
 
     mine = lax.div(me, group)
-    s_f[...], st_f[...] = slot_masks(fr_c[...], fr_r[...], experts, cap, mine)
-    s_b[...], st_b[...] = slot_masks(br_c[...], br_r[...], experts, cap, mine)
+    s_f[...], st_f[...], fw[...] = slot_masks(fr_r[...], fw_r[...], experts, cap, mine)
+    s_b[...], st_b[...], bw[...] = slot_masks(br_r[...], bw_r[...], experts, cap, mine)
     sets = ((s_f, out_f, rows_f), (s_b, out_b, rows_b), (s_b, out_g, rows_g))
     pending = []
     crossings, nears, fars = [], [], []
@@ -257,28 +276,29 @@
             weigh_into()
         place(matrix, out, into)
         cross = crossing(a, out, into)
-        for copy in cross:
-            copy.start()
         near = near_x(a, into)
-        near.start()
+        for i in range(2):
+            for copy in cross[i * (experts - 1) : (i + 1) * (experts - 1)]:
+                copy.start()
+            near[i].start()
+            send_weights(1)
         crossings.append(cross)
         nears.append(near)
-        pending += cross + [near]
+        pending += cross + near
 
     for a in range(3):
         for copy in crossings[a]:
             copy.wait_recv()
         far = far_x(a, sets[a][2])
-        far.start()
+        for copy in far:
+            copy.start()
+            send_weights(1)
         fars.append(far)
-        pending.append(far)
-    for copy in heavy:
-        copy.wait_send()
-
-    def start_down(c):
+        pending += far
+    send_weights(len(thick))
+    early = min(3, chunks)
+    for c in range(early):
         down_chunk(c).start()
-
-    each_chunk(start_down)
     for copy in local:
         copy.wait()
 
@@ -310,8 +330,8 @@
         ggr[:, pl.ds(half * hd, hd)] = (hg * upb * sig * (1.0 + pre * (1.0 - sig))).astype(BF)
         ugr[:, pl.ds(half * hd, hd)] = (hg * pre * sig).astype(BF)
 
-    nears[0].wait_recv()
-    fars[0].wait_recv()
+    for copy in nears[0] + fars[0]:
+        copy.wait_recv()
     hidden_half(0, g0, u0)
 
     def own_f(c):
@@ -319,8 +339,8 @@
 
     each_chunk(own_f)
     for a in (1, 2):
-        nears[a].wait_recv()
-        fars[a].wait_recv()
+        for copy in nears[a] + fars[a]:
+            copy.wait_recv()
     grads_start(g0, u0)
     each_chunk(functools.partial(add_t, 0))
     grads_end(0)
@@ -330,8 +350,12 @@
         sum_b[c] = part + dot_t(ugr[:, pl.ds(0, hd)], u0[col(c), :])
 
     each_chunk(own_b)
-    for copy in heavy:
-        copy.wait_recv()
+
+    def thick_in(c):
+        for kind in range(2):
+            thick_chunk(kind, c).wait_recv()
+
+    each_chunk(thick_in)
     hidden_half(1, g1, u1)
     grads_start(g1, u1)
 
@@ -364,7 +388,17 @@
         sum_f[c, pl.ds(0, rows), :] = total[:rows]
         add_t(1, c)
 
-    each_chunk(far_step_f)
+    def far_step_ahead(c, carry):
+        far_step_f(c)
+        down_chunk(c + early).start()
+        return carry
+
+    def far_step_last(c, carry):
+        far_step_f(c)
+        return carry
+
+    lax.fori_loop(0, chunks - early, far_step_ahead, 0)
+    lax.fori_loop(chunks - early, chunks, far_step_last, 0)
     grads_end(1)
 
     def far_step_b(c):
@@ -426,6 +460,8 @@
 
     def drain(c):
         down_chunk(c).wait_send()
+        for kind in range(2):
+            thick_chunk(kind, c).wait_send()
         for a in range(2):
             x_out(a, c).wait_send()
             for copy in going_back(a, c):
@@ -451,22 +487,23 @@
     scratch += [vm((chunks, tokens, cw), F32)] + [vm((chunks, tokens, cw), BF)] * 2
     scratch += [vm((tokens, width), BF), vm((tokens, 1), F32)]
     scratch += [vm((rows, tokens), BF)] * 2 + [vm((tokens, rows), BF)] * 2
-    scratch += [vm((chunks, 2 * rows, cw), F32)] * 2
-    scratch += [sem((2, 2)), sem((chunks,)), sem((chunks,)), sem((3,)), sem((3, others)), sem((3, others))]
-    scratch += [sem((3,))] * 4 + [sem((2, chunks))] * 2
+    scratch += [vm((chunks, 2 * rows, cw), F32)] * 2 + [vm((tokens, 1), F32)] * 2
+    scratch += [sem((2, chunks))] * 2 + [sem((chunks,)), sem((chunks,)), sem((3,))]
+    scratch += [sem((3, others, 2))] * 2
+    scratch += [sem((3, 2))] * 4 + [sem((2, chunks))] * 2
     scratch += [sem((2, chunks, others))] * 2 + [sem((2, chunks))] * 2
     out = jax.ShapeDtypeStruct((tokens, width), BF)
     anywhere = pl.BlockSpec(memory_space=pl.ANY)
     return pl.pallas_call(
         functools.partial(section_kernel, (experts, group, cap, chunks, cw)),
         out_shape=(out, out),
-        in_specs=[pl.BlockSpec(memory_space=vm)] * 10 + [anywhere] * 3,
+        in_specs=[pl.BlockSpec(memory_space=vm)] * 8 + [anywhere] * 3,
         out_specs=(anywhere, anywhere),
         scratch_shapes=scratch,
         compiler_params=pltpu.CompilerParams(
             collective_id=0, has_side_effects=True, vmem_limit_bytes=58 * 1024 * 1024
         ),
-    )(fi, bi, og, gain, fwt, bwt, fr, fr.T, br, br.T, gate, up, down)
+    )(fi, bi, og, gain, *[v.reshape(1, tokens) for v in (fwt, bwt, fr, br)], gate, up, down)
 
 
 def per_device(
@@ -489,7 +526,7 @@
     top = forward_route.shape[2]
     width = forward_input.shape[2]
     capacity = max(2, 3 * tokens * top // (2 * experts))
-    if top == 1 and capacity % 16 == 0 and tokens % 16 == 0 and width % 512 == 0:
+    if top == 1 and capacity % 32 == 0 and tokens % 16 == 0 and width % 512 == 0:
         next_input, previous_grad = fused(
             forward_input[0], forward_route[0], forward_weight[0],
             backward_input[0], backward_route[0], backward_weight[0],

time: 257 us -> 253 us (0.984)
  local copies, waits for them, and re-layouts: 8.69 us -> 3.17 us
    squeeze x4 -> x0, local copies, waits for them, and re-layouts: 5.53 us -> none  [the longest x1 1.39 us: per_device(): forward_weight[0]]
where the time goes in v5:
time: 253 us; the launch traced here: 252 us
  Pallas kernels  249 us (98%)
  local copies, waits for them, and re-layouts  3.17 us (1%)
    pallas_call x1, Pallas kernels, fused(): pl.pallas_call(functools.partial(section_kernel, (experts, group, cap, ch...  249 us

profile of v5, /device:TPU:1, one launch (start us, length us, event | category | flops | bytes accessed | tf_op | source)
XLA Modules:
  0.0 252.5 jit_solution(15563893823893854335)
XLA Ops:
  0.6 248.6 %shard_map.122 = (bf16[128,3584]{1,0:T(8,128)(2,1)}, bf16[128,3584]{1,0:T(8,128)(2,1)}) custom-call(bf16[128,3584]{1,0:T(8,128)(2,1)} %bitcast.17, bf16[128,3584]{1,0:T(8,128)(2,1)} %bitcast.18, bf16[128,3584]{1,0:T(8,128)(2,1)} %bitcast.19, f32[1,3584]{1,0:T(1,128)} %gain.1, f32[1,128]{1,0:T(1,128)} %bitcast.20, f32[1,128]{1,0:T(1,128)} %bitcast.21, ...), custom_call_target="tpu_custom_call" | custom-call | tf_op jit(solution)/shard_map/pallas_call | solution.py:497
  249.3 0.0 copy-start
  249.3 2.2 copy.15
  251.5 0.0 copy-done
  251.5 0.9 copy.16
Async XLA Ops:
  249.3 2.3 copy-start

commit v6 on v5

--- a/solution.py
+++ b/solution.py
@@ -286,7 +286,35 @@
         nears.append(near)
         pending += cross + near
 
-    for a in range(3):
+    def first(source, weight, acc):
+        acc[...] = jnp.zeros_like(acc)
+
+        def body(c):
+            acc[...] += dot(source[:, col(c)], weight[col(c), :])
+
+        each_chunk(body)
+
+    def add_t(half, c):
+        acc_c[...] += dot_t(rows_g[:, col(c)], dd[pl.ds(half * hd, hd), col(c)])
+
+    def hidden_half(half, gw, uw):
+        first(rows_f, gw, acc_a)
+        first(rows_f, uw, acc_b)
+        pre = acc_a[...]
+        hid[:, pl.ds(half * hd, hd)] = (pre * jax.nn.sigmoid(pre) * acc_b[...]).astype(BF)
+
+    def grads_start(gw, uw):
+        first(rows_b, gw, acc_a)
+        first(rows_b, uw, acc_b)
+        acc_c[...] = jnp.zeros_like(acc_c)
+
+    def grads_end(half):
+        pre, upb, hg = acc_a[...], acc_b[...], acc_c[...]
+        sig = jax.nn.sigmoid(pre)
+        ggr[:, pl.ds(half * hd, hd)] = (hg * upb * sig * (1.0 + pre * (1.0 - sig))).astype(BF)
+        ugr[:, pl.ds(half * hd, hd)] = (hg * pre * sig).astype(BF)
+
+    def forward_on(a):
         for copy in crossings[a]:
             copy.wait_recv()
         far = far_x(a, sets[a][2])
@@ -294,54 +322,32 @@
             copy.start()
             send_weights(1)
         fars.append(far)
-        pending += far
+        pending.extend(far)
+
+    def all_in(a):
+        for copy in nears[a] + fars[a]:
+            copy.wait_recv()
+
+    forward_on(0)
+    for copy in local:
+        copy.wait()
+    forward_on(1)
+    all_in(0)
+    hidden_half(0, g0, u0)
+
+    def own_f(c):
+        sum_f[c] = dot(hid[:, pl.ds(0, hd)], dd[pl.ds(0, hd), col(c)])
+
+    each_chunk(own_f)
+    send_weights(1)
+    all_in(1)
+    grads_start(g0, u0)
+    forward_on(2)
     send_weights(len(thick))
-    early = min(3, chunks)
+    early = min(5, chunks)
     for c in range(early):
         down_chunk(c).start()
-    for copy in local:
-        copy.wait()
-
-    def first(source, weight, acc):
-        acc[...] = jnp.zeros_like(acc)
-
-        def body(c):
-            acc[...] += dot(source[:, col(c)], weight[col(c), :])
-
-        each_chunk(body)
-
-    def add_t(half, c):
-        acc_c[...] += dot_t(rows_g[:, col(c)], dd[pl.ds(half * hd, hd), col(c)])
-
-    def hidden_half(half, gw, uw):
-        first(rows_f, gw, acc_a)
-        first(rows_f, uw, acc_b)
-        pre = acc_a[...]
-        hid[:, pl.ds(half * hd, hd)] = (pre * jax.nn.sigmoid(pre) * acc_b[...]).astype(BF)
-
-    def grads_start(gw, uw):
-        first(rows_b, gw, acc_a)
-        first(rows_b, uw, acc_b)
-        acc_c[...] = jnp.zeros_like(acc_c)
-
-    def grads_end(half):
-        pre, upb, hg = acc_a[...], acc_b[...], acc_c[...]
-        sig = jax.nn.sigmoid(pre)
-        ggr[:, pl.ds(half * hd, hd)] = (hg * upb * sig * (1.0 + pre * (1.0 - sig))).astype(BF)
-        ugr[:, pl.ds(half * hd, hd)] = (hg * pre * sig).astype(BF)
-
-    for copy in nears[0] + fars[0]:
-        copy.wait_recv()
-    hidden_half(0, g0, u0)
-
-    def own_f(c):
-        sum_f[c] = dot(hid[:, pl.ds(0, hd)], dd[pl.ds(0, hd), col(c)])
-
-    each_chunk(own_f)
-    for a in (1, 2):
-        for copy in nears[a] + fars[a]:
-            copy.wait_recv()
-    grads_start(g0, u0)
+    all_in(2)
     each_chunk(functools.partial(add_t, 0))
     grads_end(0)
 

time: 253 us -> 253 us (level)
  no operation moved by 1% of the time
where the time goes in v6:
time: 253 us; the launch traced here: 252 us
  Pallas kernels  249 us (98%)
  local copies, waits for them, and re-layouts  3.17 us (1%)
    pallas_call x1, Pallas kernels, fused(): pl.pallas_call(functools.partial(section_kernel, (experts, group, cap, ch...  249 us

profile of v6, /device:TPU:1, one launch (start us, length us, event | category | flops | bytes accessed | tf_op | source)
XLA Modules:
  0.0 252.5 jit_solution(8042167012583547206)
XLA Ops:
  0.6 248.6 %shard_map.122 = (bf16[128,3584]{1,0:T(8,128)(2,1)}, bf16[128,3584]{1,0:T(8,128)(2,1)}) custom-call(bf16[128,3584]{1,0:T(8,128)(2,1)} %bitcast.17, bf16[128,3584]{1,0:T(8,128)(2,1)} %bitcast.18, bf16[128,3584]{1,0:T(8,128)(2,1)} %bitcast.19, f32[1,3584]{1,0:T(1,128)} %gain.1, f32[1,128]{1,0:T(1,128)} %bitcast.20, f32[1,128]{1,0:T(1,128)} %bitcast.21, ...), custom_call_target="tpu_custom_call" | custom-call | tf_op jit(solution)/shard_map/pallas_call | solution.py:503
  249.3 0.0 copy-start
  249.3 2.2 copy.15
  251.5 0.0 copy-done
  251.5 0.9 copy.16
Async XLA Ops:
  249.3 2.3 copy-start
